TPU v7x, 512 devices: a whole 4x8x8 slice. The times are simulated.
512 devices in a mesh: face: 4 (over z_hi), tile: 128 (over x, z_lo, y, core).
Axes of the slice: x: 4, y: 8, z: 8 (z_hi: 4, z_lo: 2; z = z_hi * 2 + z_lo), core: 2. Of those that a mesh axis runs over, the one named last changes fastest.
Arguments:
- sample: bfloat16 [12, 1024, 32, 192], P('face', 'tile'), may hold values from -6 to 6
- noise_field: bfloat16 [12, 1024, 32, 192], P('face', 'tile'), may hold values from -6 to 6
- coarse_state: bfloat16 [12, 128, 4, 192], P('face', 'tile'), may hold values from -6 to 6
- first_kernel: bfloat16 [3, 3, 384, 192], replicated, may hold values from -0.109375 to 0.109375
- first_bias: float32 [192], replicated, may hold values from -3 to 3
- second_kernel: bfloat16 [3, 3, 192, 192], replicated, may hold values from -0.15625 to 0.15625
- second_bias: float32 [192], replicated, may hold values from -3 to 3
- ns_neighbour: int32 [12, 2], replicated, may hold values from 0 to 2
- we_neighbour: int32 [12, 2], replicated, may hold values from 0 to 11
- edge_code: int32 [12, 4], replicated, may hold values from 0 to 1
Outputs:
- next_sample: bfloat16 [12, 1024, 32, 192], P('face', 'tile')
Inputs may be any that keep to these rules, and one draw needn't show every extreme that they name: ns_neighbour counts within the face's own group: it names face 3 (f // 3) + value.
All inputs are finite; a program needn't handle non-finite values.
Results may differ from a plain program's by a relative error of at most 0.0022.
Values may be sent and summed in bfloat16 or wider, within the bound.
A program may use at most 64 MiB of HBM per device.

v0:
```python
import jax
import jax.numpy as jnp
from jax import lax
from jax.sharding import PartitionSpec as P

UP = 8


noise_gain = 0.6
input_gain = 0.7071067811865476
skip_gain = 0.5
output_gain = 0.7071067811865476
step_ratio = -0.4


def extended(x, sides, width):
    for axis, dim in sides:
        size, length = (lax.axis_size(axis), x.shape[dim])
        up = [(i, (i + 1) % size) for i in range(size)]
        down = [(j, i) for i, j in up]
        last = lax.slice_in_dim(x, length - width, length, axis=dim)
        leading = lax.slice_in_dim(x, 0, width, axis=dim)
        before = lax.ppermute(last, axis, up)
        after = lax.ppermute(leading, axis, down)
        x = jnp.concatenate([before, x, after], axis=dim)
    return x


def pick_rims(indices, rim_table):
    size = rim_table.shape[0]
    selector = (indices[:, None] == jnp.arange(size, dtype=jnp.int32)[None, :]).astype(
        rim_table.dtype
    )
    flat = rim_table.reshape(size, -1)
    chosen = jnp.dot(selector, flat, preferred_element_type=jnp.float32).astype(rim_table.dtype)
    return chosen.reshape((indices.shape[0],) + rim_table.shape[1:])


def pad_fields(fields, ns_neighbour, we_neighbour, edge_code):
    group_index = lax.axis_index("face")
    position = lax.axis_index("tile")
    last_tile = lax.axis_size("tile") - 1
    face_count = fields[0].shape[0]
    first_face = group_index * face_count
    ns_local = lax.dynamic_slice(ns_neighbour, (first_face, 0), (face_count, 2))
    we_local = lax.dynamic_slice(we_neighbour, (first_face, 0), (face_count, 2))
    local_codes = lax.dynamic_slice(edge_code, (first_face, 0), (face_count, 4))
    top_rims = jnp.concatenate([one_field[:, 0] for one_field in fields], axis=1)
    bottom_rims = jnp.concatenate([one_field[:, -1] for one_field in fields], axis=1)
    edge_rows = jnp.stack([top_rims, bottom_rims], axis=1)
    haloed = extended(edge_rows, (("tile", 1),), 1)
    from_above = haloed[:, 0]
    from_below = haloed[:, 3]
    north_rims = jnp.where(position == 0, top_rims, from_below)
    south_rims = jnp.where(position == last_tile, bottom_rims, from_above)
    own_table = jnp.stack([north_rims, south_rims], axis=1).reshape(
        (2 * face_count,) + top_rims.shape[1:]
    )
    cross_north = pick_rims(ns_local[:, 0] * 2 + 1 - local_codes[:, 0], own_table)
    cross_south = pick_rims(ns_local[:, 1] * 2 + local_codes[:, 1], own_table)
    top_rows = jnp.where(position == 0, cross_north, from_above)
    bottom_rows = jnp.where(position == last_tile, cross_south, from_below)
    row_padded_list = []
    west_parts = []
    east_parts = []
    offset = 0
    for one_field in fields:
        width = one_field.shape[2]
        row_padded = jnp.concatenate([top_rows[:, None], one_field, bottom_rows[:, None]], axis=1)
        row_padded_list.append(row_padded)
        west_parts.append(row_padded[:, :, 0])
        east_parts.append(row_padded[:, :, -1])
        offset = offset + width
    side_cols = jnp.stack([west_parts[0], east_parts[0]], axis=1)
    everyone = lax.all_gather(side_cols, "face", axis=0, tiled=True)
    all_table = everyone.reshape((everyone.shape[0] * 2,) + side_cols.shape[2:])
    cross_west = pick_rims(we_local[:, 0] * 2 + 1 - local_codes[:, 2], all_table)
    cross_east = pick_rims(we_local[:, 1] * 2 + local_codes[:, 3], all_table)
    offset = 0
    row_padded = row_padded_list[0]
    height = row_padded.shape[1]
    row_index = jnp.arange(height, dtype=jnp.int32)
    keep = jnp.logical_not(
        jnp.logical_or(
            jnp.logical_and(row_index == 0, position == 0),
            jnp.logical_and(row_index == height - 1, position == last_tile),
        )
    )
    keep = keep.astype(row_padded.dtype)[None, :, None]
    west_col = cross_west * keep
    east_col = cross_east * keep
    padded_list = [
        jnp.concatenate([west_col[:, :, None], row_padded, east_col[:, :, None]], axis=2)
    ]
    return padded_list


def convolve(padded, kernel):
    face_total = padded.shape[0]
    row_count = padded.shape[1] - 2
    col_count = padded.shape[2] - 2
    width_in = padded.shape[3]
    width_out = kernel.shape[3]
    accumulated = jnp.zeros((face_total * row_count * col_count, width_out), jnp.float32)
    for shift_row in range(3):
        for shift_col in range(3):
            window = padded[:, shift_row : shift_row + row_count, shift_col : shift_col + col_count]
            accumulated = accumulated + jnp.dot(
                window.reshape(face_total * row_count * col_count, width_in),
                kernel[shift_row, shift_col],
                preferred_element_type=jnp.float32,
            )
    return accumulated.reshape(face_total, row_count, col_count, width_out)


def on_device(
    sample,
    noise_field,
    coarse_state,
    first_kernel,
    first_bias,
    second_kernel,
    second_bias,
    ns_neighbour,
    we_neighbour,
    edge_code,
):
    perturbed = sample.astype(jnp.float32) + noise_gain * noise_field.astype(jnp.float32)
    net_input = (perturbed * input_gain).astype(jnp.bfloat16)
    upsampled = jnp.repeat(jnp.repeat(coarse_state, UP, axis=1), UP, axis=2)
    mixed_input = jnp.concatenate([net_input, upsampled], axis=-1)
    padded_mixed = pad_fields([mixed_input], ns_neighbour, we_neighbour, edge_code)[0]
    activation = convolve(padded_mixed, first_kernel)
    hidden = jax.nn.silu(activation + first_bias).astype(jnp.bfloat16)
    padded_hidden = pad_fields([hidden], ns_neighbour, we_neighbour, edge_code)[0]
    feature = convolve(padded_hidden, second_kernel) + second_bias
    denoised = skip_gain * perturbed + output_gain * feature
    result = perturbed + step_ratio * (perturbed - denoised)
    return result.astype(jnp.bfloat16)


def solution(mesh):
    return jax.shard_map(
        on_device,
        mesh=mesh,
        in_specs=(
            P("face", "tile", None, None),
            P("face", "tile", None, None),
            P("face", "tile", None, None),
            P(),
            P(),
            P(),
            P(),
            P(),
            P(),
            P(),
        ),
        out_specs=P("face", "tile", None, None),
        check_vma=False,
    )
```

profile of v0, /device:TPU:128, one launch (start us, length us, event | category | flops | bytes accessed | tf_op | source)
XLA Modules:
  0.0 80.0 jit_solution(6463563055405094617)
XLA Ops:
  0.0 0.7 copy-done
  0.7 1.3 %multiply_convert_fusion.1 = bf16[3,8,32,192]{3,2,1,0:T(8,128)(2,1)S(1)} fusion(bf16[3,8,32,192]{3,2,1,0:T(8,128)(2,1)} %param.11, bf16[3,8,32,192]{3,2,1,0:T(8,128)(2,1)} %param.10), kind=kLoop, calls=%fused_computation.28 | loop fusion | flops 884736 | bytes 884736 | tf_op jit(solution)/shard_map/convert_element_type | solution.py:129
  2.1 8.8 %collective-permute-start = (bf16[3,1,32,384]{3,2,1,0:T(8,128)(2,1)S(1)}, bf16[3,1,32,384]{3,2,1,0:T(8,128)(2,1)S(1)}, u32[]{:S(2)}, u32[]{:S(2)}) collective-permute-start(bf16[3,1,32,384]{3,2,1,0:T(8,128)(2,1)S(1)} %get-tuple-element.18), channel_id=1, source_target_pairs={{1,0},{2,1},{3,2},{4,3},{5,4},{6,5},{7,6},{8,7},{9,8},{10,9},{11,1... | collective-permute-start | bytes 221192 | tf_op jit(solution)/shard_map/ppermute | solution.py:24
  11.0 1.9 %collective-permute-start.1 = (bf16[3,1,32,384]{3,2,1,0:T(8,128)(2,1)S(1)}, bf16[3,1,32,384]{3,2,1,0:T(8,128)(2,1)S(1)}, u32[]{:S(2)}, u32[]{:S(2)}) collective-permute-start(bf16[3,1,32,384]{3,2,1,0:T(8,128)(2,1)S(1)} %get-tuple-element.17), channel_id=1, source_target_pairs={{0,1},{1,2},{2,3},{3,4},{4,5},{5,6},{6,7},{7,8},{8,9},{9,10},{10,1... | collective-permute-start | bytes 221192 | tf_op jit(solution)/shard_map/ppermute | solution.py:23
  13.1 7.7 %collective-permute-done.1 = bf16[3,1,32,384]{3,2,1,0:T(8,128)(2,1)S(1)} collective-permute-done((bf16[3,1,32,384]{3,2,1,0:T(8,128)(2,1)S(1)}, bf16[3,1,32,384]{3,2,1,0:T(8,128)(2,1)S(1)}, u32[]{:S(2)}, u32[]{:S(2)}) %collective-permute-start.1) | collective-permute-done | bytes 73760 | tf_op jit(solution)/shard_map/ppermute | solution.py:23
  21.7 0.4 pad_maximum_fusion.2
  22.2 16.7 %all_gather.6 = bf16[12,2,10,384]{3,1,2,0:T(2,128)(2,1)S(1)} all-gather(bf16[3,2,10,384]{3,1,2,0:T(2,128)(2,1)S(1)} %copy.121), channel_id=1, replica_groups=mesh['face'=4,'tile'=128] {'face'}, dimensions={0}, use_global_device_ids=true | all-gather | bytes 230400 | tf_op jit(solution)/shard_map/all_gather | solution.py:75
  39.7 0.7 pad_maximum_fusion
  40.6 0.3 fusion.53
  41.0 1.0 %copy-done.3 = bf16[3,3,384,192]{2,3,1,0:T(8,128)(2,1)S(1)} copy-done((bf16[3,3,384,192]{2,3,1,0:T(8,128)(2,1)S(1)}, bf16[3,3,384,192]{2,3,1,0:T(8,128)(2,1)}, u32[]{:S(2)}) %copy-start.3) | copy-done | bytes 1327128
  41.9 0.4 fusion.13
  42.3 0.4 convolution_add_fusion.15
  42.7 0.4 convolution_add_fusion.14
  43.0 0.4 convolution_add_fusion.13
  43.4 0.4 convolution_add_fusion.12
  43.9 0.4 convolution_add_fusion.11
  44.2 0.4 convolution_add_fusion.10
  44.6 0.4 convolution_add_fusion.9
  45.0 0.4 convolution_add_fusion.8
  45.9 1.9 %collective-permute-start.2 = (bf16[3,1,32,192]{3,2,1,0:T(8,128)(2,1)S(1)}, bf16[3,1,32,192]{3,2,1,0:T(8,128)(2,1)S(1)}, u32[]{:S(2)}, u32[]{:S(2)}) collective-permute-start(bf16[3,1,32,192]{3,2,1,0:T(8,128)(2,1)S(1)} %get-tuple-element.34), channel_id=1, source_target_pairs={{1,0},{2,1},{3,2},{4,3},{5,4},{6,5},{7,6},{8,7},{9,8},{10,9},{11,1... | collective-permute-start | bytes 110600 | tf_op jit(solution)/shard_map/ppermute | solution.py:24
  47.8 2.4 %collective-permute-start.3 = (bf16[3,1,32,192]{3,2,1,0:T(8,128)(2,1)S(1)}, bf16[3,1,32,192]{3,2,1,0:T(8,128)(2,1)S(1)}, u32[]{:S(2)}, u32[]{:S(2)}) collective-permute-start(bf16[3,1,32,192]{3,2,1,0:T(8,128)(2,1)S(1)} %get-tuple-element.33), channel_id=1, source_target_pairs={{0,1},{1,2},{2,3},{3,4},{4,5},{5,6},{6,7},{7,8},{8,9},{9,10},{10,1... | collective-permute-start | bytes 110600 | tf_op jit(solution)/shard_map/ppermute | solution.py:23
  50.2 7.4 %collective-permute-done.3 = bf16[3,1,32,192]{3,2,1,0:T(8,128)(2,1)S(1)} collective-permute-done((bf16[3,1,32,192]{3,2,1,0:T(8,128)(2,1)S(1)}, bf16[3,1,32,192]{3,2,1,0:T(8,128)(2,1)S(1)}, u32[]{:S(2)}, u32[]{:S(2)}) %collective-permute-start.3) | collective-permute-done | bytes 36896 | tf_op jit(solution)/shard_map/ppermute | solution.py:23
  58.9 13.8 %all_gather.7 = bf16[12,2,10,192]{3,1,2,0:T(2,128)(2,1)S(1)} all-gather(bf16[3,2,10,192]{3,1,2,0:T(2,128)(2,1)S(1)} %copy.130), channel_id=1, replica_groups=mesh['face'=4,'tile'=128] {'face'}, dimensions={0}, use_global_device_ids=true | all-gather | bytes 115200 | tf_op jit(solution)/shard_map/all_gather | solution.py:75
  73.6 0.3 pad_maximum_fusion.1
  74.2 0.9 %copy-done.4 = bf16[3,3,192,192]{3,2,1,0:T(8,128)(2,1)S(1)} copy-done((bf16[3,3,192,192]{3,2,1,0:T(8,128)(2,1)S(1)}, bf16[3,3,192,192]{3,2,1,0:T(8,128)(2,1)}, u32[]{:S(2)}) %copy-start.4) | copy-done | bytes 663576
  75.5 0.3 convolution_add_fusion.7
  76.1 0.3 convolution_add_fusion.5
  76.4 0.4 convolution_add_fusion.4
  77.2 0.3 convolution_add_fusion.2
  77.5 0.3 convolution_add_fusion.1
  78.4 0.4 copy-done.1
  78.9 1.1 %add_convert_fusion = bf16[3,8,32,192]{3,2,1,0:T(8,128)(2,1)} fusion(f32[3,8,32,192]{3,2,1,0:T(8,128)S(1)} %bitcast.144, bf16[3,8,32,192]{3,2,1,0:T(8,128)(2,1)S(1)} %copy-done.1, bf16[3,8,32,192]{3,2,1,0:T(8,128)(2,1)S(1)} %copy-done.2, f32[192]{0:T(256)S(1)} %copy-done.6), kind=kLoop, calls=%fused_computation.26 | loop fusion | flops 1769472 | bytes 1475328 | tf_op jit(solution)/shard_map/convert_element_type | solution.py:139
  (78 shorter events, 6.7 us)
Async XLA Ops:
  0.0 0.7 copy-start
  0.0 12.9 %copy-start.5 = (s32[12,4]{0,1:T(4,128)S(1)}, s32[12,4]{0,1:T(4,128)}, u32[]{:S(2)}) copy-start(s32[12,4]{0,1:T(4,128)} %param.19) | copy-start | bytes 580
  0.0 13.0 %copy-start.7 = (s32[12,2]{0,1:T(2,128)S(1)}, s32[12,2]{0,1:T(2,128)}, u32[]{:S(2)}) copy-start(s32[12,2]{0,1:T(2,128)} %param.17) | copy-start | bytes 292
  0.0 13.0 %copy-start.8 = (s32[12,2]{0,1:T(2,128)S(1)}, s32[12,2]{0,1:T(2,128)}, u32[]{:S(2)}) copy-start(s32[12,2]{0,1:T(2,128)} %param.18) | copy-start | bytes 292
  2.1 11.0 %collective-permute-start = (bf16[3,1,32,384]{3,2,1,0:T(8,128)(2,1)S(1)}, bf16[3,1,32,384]{3,2,1,0:T(8,128)(2,1)S(1)}, u32[]{:S(2)}, u32[]{:S(2)}) collective-permute-start(bf16[3,1,32,384]{3,2,1,0:T(8,128)(2,1)S(1)} %get-tuple-element.18), channel_id=1, source_target_pairs={{1,0},{2,1},{3,2},{4,3},{5,4},{6,5},{7,6},{8,7},{9,8},{10,9},{11,1... | collective-permute-start | bytes 221192 | tf_op jit(solution)/shard_map/ppermute | solution.py:24
  11.0 9.9 %collective-permute-start.1 = (bf16[3,1,32,384]{3,2,1,0:T(8,128)(2,1)S(1)}, bf16[3,1,32,384]{3,2,1,0:T(8,128)(2,1)S(1)}, u32[]{:S(2)}, u32[]{:S(2)}) collective-permute-start(bf16[3,1,32,384]{3,2,1,0:T(8,128)(2,1)S(1)} %get-tuple-element.17), channel_id=1, source_target_pairs={{0,1},{1,2},{2,3},{3,4},{4,5},{5,6},{6,7},{7,8},{8,9},{9,10},{10,1... | collective-permute-start | bytes 221192 | tf_op jit(solution)/shard_map/ppermute | solution.py:23
  40.6 1.3 %copy-start.3 = (bf16[3,3,384,192]{2,3,1,0:T(8,128)(2,1)S(1)}, bf16[3,3,384,192]{2,3,1,0:T(8,128)(2,1)}, u32[]{:S(2)}) copy-start(bf16[3,3,384,192]{2,3,1,0:T(8,128)(2,1)} %param.13) | copy-start | bytes 3981316
  45.0 0.7 copy-start.9
  45.9 4.3 %collective-permute-start.2 = (bf16[3,1,32,192]{3,2,1,0:T(8,128)(2,1)S(1)}, bf16[3,1,32,192]{3,2,1,0:T(8,128)(2,1)S(1)}, u32[]{:S(2)}, u32[]{:S(2)}) collective-permute-start(bf16[3,1,32,192]{3,2,1,0:T(8,128)(2,1)S(1)} %get-tuple-element.34), channel_id=1, source_target_pairs={{1,0},{2,1},{3,2},{4,3},{5,4},{6,5},{7,6},{8,7},{9,8},{10,9},{11,1... | collective-permute-start | bytes 110600 | tf_op jit(solution)/shard_map/ppermute | solution.py:24
  47.8 9.8 %collective-permute-start.3 = (bf16[3,1,32,192]{3,2,1,0:T(8,128)(2,1)S(1)}, bf16[3,1,32,192]{3,2,1,0:T(8,128)(2,1)S(1)}, u32[]{:S(2)}, u32[]{:S(2)}) collective-permute-start(bf16[3,1,32,192]{3,2,1,0:T(8,128)(2,1)S(1)} %get-tuple-element.33), channel_id=1, source_target_pairs={{0,1},{1,2},{2,3},{3,4},{4,5},{5,6},{6,7},{7,8},{8,9},{9,10},{10,1... | collective-permute-start | bytes 110600 | tf_op jit(solution)/shard_map/ppermute | solution.py:23
  74.0 1.2 %copy-start.4 = (bf16[3,3,192,192]{3,2,1,0:T(8,128)(2,1)S(1)}, bf16[3,3,192,192]{3,2,1,0:T(8,128)(2,1)}, u32[]{:S(2)}) copy-start(bf16[3,3,192,192]{3,2,1,0:T(8,128)(2,1)} %param.15) | copy-start | bytes 1990660
  77.8 1.0 %copy-start.1 = (bf16[3,8,32,192]{3,2,1,0:T(8,128)(2,1)S(1)}, bf16[3,8,32,192]{3,2,1,0:T(8,128)(2,1)}, u32[]{:S(2)}) copy-start(bf16[3,8,32,192]{3,2,1,0:T(8,128)(2,1)} %param.11) | copy-start | bytes 884740
  77.8 1.1 %copy-start.2 = (bf16[3,8,32,192]{3,2,1,0:T(8,128)(2,1)S(1)}, bf16[3,8,32,192]{3,2,1,0:T(8,128)(2,1)}, u32[]{:S(2)}) copy-start(bf16[3,8,32,192]{3,2,1,0:T(8,128)(2,1)} %param.10) | copy-start | bytes 884740
  77.8 1.1 %copy-start.6 = (f32[192]{0:T(256)S(1)}, f32[192]{0:T(256)}, u32[]{:S(2)}) copy-start(f32[192]{0:T(256)} %param.16) | copy-start | bytes 2308
where the time goes:
time: 80.3 us; the launch traced here: 80 us
  blocking collectives  30.5 us (38%)
  starting transfers between devices  15.1 us (19%)
  waiting for transfers between devices  15.1 us (19%)
  matrix products  8 us (10%)
  local copies, waits for them, and re-layouts  5.85 us (7%)
  other arithmetic  4.86 us (6%)
    all_gather x2, blocking collectives, pad_fields(): everyone = lax.all_gather(side_cols, 'face', axis=0, tiled=True)  30.5 us
    ppermute x2, waiting for transfers between devices, extended(): before = lax.ppermute(last, axis, up)  15.1 us
    ppermute x2, starting transfers between devices, extended(): after = lax.ppermute(leading, axis, down)  10.7 us
    dot_general x18, matrix products, convolve(): jnp.dot(window.reshape(face_total * row_count * col_count, width_in), ker...  6.23 us
    ppermute x2, starting transfers between devices, extended(): before = lax.ppermute(last, axis, up)  4.33 us
    unnamed x22, local copies, waits for them, and re-layouts  3.24 us
    dot_general x8, matrix products, pick_rims(): jnp.dot(selector, flat, preferred_element_type=jnp.float32)  1.76 us
  transfers between devices with their start and end apart: 4, of which 2 were waited for; matrix products, arithmetic and copies ran while one was open for 0% of the time, Pallas kernels for 0%

commit v1 on v0

v1 whole, which is shorter than its diff:
```python
import functools

import jax
import jax.numpy as jnp
from jax import lax
from jax.experimental import pallas as pl
from jax.experimental.pallas import tpu as pltpu
from jax.sharding import PartitionSpec as P

MESH = pl.DeviceIdType.MESH
f32 = jnp.float32
bf16 = jnp.bfloat16

noise_gain = 0.6
input_gain = 0.7071067811865476
skip_gain = 0.5
output_gain = 0.7071067811865476
step_ratio = -0.4

UP = 8
FACES = 3
ROWS = 8
COLS = 32
COARSE = COLS // UP
PIX = ROWS * COLS
BLOCKS = 6


def dot(a, b):
    return jnp.dot(a, b, preferred_element_type=f32)


def column_of(shape):
    return lax.rem(lax.broadcasted_iota(jnp.int32, shape, 0), COLS)


def from_west(z):
    return jnp.where(column_of(z.shape) == 0, 0.0, pltpu.roll(z, 1, 0))


def from_east(z):
    return jnp.where(column_of(z.shape) == COLS - 1, 0.0, pltpu.roll(z, z.shape[0] - 1, 0))


def along_rows(v0, v1, v2):
    return pltpu.roll(v0, 1, 0) + v1 + pltpu.roll(v2, v2.shape[0] - 1, 0)


def spread(rows, count=16):
    width = rows[0][1].shape[1]
    place = lax.broadcasted_iota(jnp.int32, (count, width), 0)
    out = jnp.zeros((count, width), f32)
    for at, row in rows:
        out = jnp.where(place == at, jnp.broadcast_to(row, (count, width)), out)
    return out


def kernel(
    groups,
    tiles,
    sample_hbm,
    noise_hbm,
    coarse_hbm,
    w1_hbm,
    w2_hbm,
    b1,
    b2,
    ns,
    we,
    code,
    out,
    sample,
    noise,
    coarse,
    w1,
    w2,
    pf,
    acc,
    xp,
    hp,
    up,
    cclass,
    cols1,
    cols2,
    corner1,
    corner2,
    rows1,
    rows2,
    pick,
    zcol,
    zrow,
    load_sem,
    send_sem,
    recv_sem,
):
    g = lax.axis_index("face")
    t = lax.axis_index("tile")
    above = lax.rem(t + tiles - 1, tiles)
    below = lax.rem(t + 1, tiles)
    first = t == 0
    last = t == tiles - 1
    C = pf.shape[2]

    loads = [
        pltpu.make_async_copy(src, dst, load_sem.at[i])
        for i, (src, dst) in enumerate(
            [(sample_hbm, sample), (noise_hbm, noise), (coarse_hbm, coarse), (w1_hbm, w1), (w2_hbm, w2)]
        )
    ]
    for copy in loads:
        copy.start()

    barrier = pltpu.get_barrier_semaphore()
    for d in range(groups):
        for k, there in enumerate((t, above, below)):
            if d or k:
                pl.semaphore_signal(
                    barrier, inc=1, device_id=(lax.rem(g + d, groups), there), device_id_type=MESH
                )

    def copies(stage, cols, corner, rows):
        made = []

        def add(src, dst, there):
            n = len(made)
            made.append(
                pltpu.make_async_remote_copy(
                    src_ref=src,
                    dst_ref=dst,
                    send_sem=send_sem.at[stage, n],
                    recv_sem=recv_sem.at[stage, n],
                    device_id=there,
                    device_id_type=MESH,
                )
            )

        for d in (2, 1, 3):
            far = lax.rem(g + d, groups)
            table = pl.ds(0, 4) if stage == 0 else pl.ds(1, 3)
            add(cols.at[g, table], cols.at[g, table], (far, t))
            add(corner.at[0], cols.at[g, 5], (far, above))
            add(corner.at[1], cols.at[g, 4], (far, below))
        add(rows.at[2], rows.at[1], (g, above))
        add(rows.at[3], rows.at[0], (g, below))
        add(corner.at[0], cols.at[g, 5], (g, above))
        add(corner.at[1], cols.at[g, 4], (g, below))
        return made

    lane = lax.broadcasted_iota(jnp.int32, (16, groups * BLOCKS * 16), 1)
    place = lax.broadcasted_iota(jnp.int32, (16, groups * BLOCKS * 16), 0)
    for side in range(2):
        for f in range(FACES):
            face = g * FACES + f
            src = we[face, side]
            edge = code[face, 2 + side]
            src_side = edge if side else 1 - edge
            src_g = (
                (src >= 3).astype(jnp.int32) + (src >= 6).astype(jnp.int32) + (src >= 9).astype(jnp.int32)
            )
            src_f = src - 3 * src_g
            base = src_g * (BLOCKS * 16)
            near = base + 4 * 16 + src_f * 2 + src_side
            for part in range(2):
                over = jnp.where(first, -1, near + 8 * part)
                under = jnp.where(last, -1, near + 16 + 8 * part)
                if part == 0:
                    inner = base + (1 + src_f) * 16 + src_side * 8 + place - 1
                else:
                    inner = jnp.broadcast_to(base + src_f * 4 + src_side * 3, place.shape)
                target = jnp.where(place == 0, over, jnp.where(place == ROWS + 1, under, inner))
                target = jnp.where(place > ROWS + 1, -1, target)
                at = part * 96 + side * 48 + f * 16
                pick[at : at + 16, :] = jnp.where(lane == target, 1.0, 0.0).astype(bf16)

    zero_row = jnp.zeros((COLS, C), bf16)
    for f in range(FACES):
        for ref in (xp, hp):
            ref[f, 0:COLS] = zero_row
            ref[f, COLS + PIX : 2 * COLS + PIX] = zero_row
    for d in range(groups):
        cols2[d, 0] = jnp.zeros((16, C), bf16)

    def fill_tables(values, gain, cols, corner, extra):
        tops, ends = [], []
        for f in range(FACES):
            lines = [[values[f, i * COLS + j : i * COLS + j + 1, :] for i in range(ROWS)] for j in (0, COLS - 1)]
            west, east = [spread(list(enumerate(line)), ROWS) * gain for line in lines]
            cols[g, 1 + f] = jnp.concatenate([west, east], axis=0).astype(bf16)
            tops += [(2 * f, west[0:1]), (2 * f + 1, east[0:1])]
            ends += [(2 * f, west[ROWS - 1 : ROWS]), (2 * f + 1, east[ROWS - 1 : ROWS])]
        corner[0] = spread(tops + extra).astype(bf16)
        corner[1] = spread(ends + extra).astype(bf16)

    for copy in loads[:3]:
        copy.wait()
    for f in range(FACES):
        p = sample[f].astype(f32) + noise_gain * noise[f].astype(f32)
        p = p.reshape(PIX, C)
        pf[f] = p
        net = (p * input_gain).astype(bf16)
        xp[f, COLS : COLS + PIX] = net
        rows1[2, f, 0] = net[0:COLS]
        rows1[3, f, 0] = net[PIX - COLS : PIX]
    raw, edges = [], []
    for f in range(FACES):
        c = coarse[f, 0].astype(f32)
        each = [c[j : j + 1] for j in range(COARSE)]
        raw += [(4 * f + j, each[j]) for j in range(COARSE)]
        edges += [(8 + 2 * f, each[0]), (9 + 2 * f, each[COARSE - 1])]
        wide = jnp.concatenate([jnp.broadcast_to(e, (UP, C)) for e in each], axis=0).astype(bf16)
        up[f * COLS : (f + 1) * COLS] = wide
        rows1[2, f, 1] = wide
        rows1[3, f, 1] = wide
    cols1[g, 0] = spread(raw).astype(bf16)
    fill_tables(pf, input_gain, cols1, corner1, edges)

    pl.semaphore_wait(barrier, 3 * groups - 1)
    sent1 = copies(0, cols1, corner1, rows1)
    for copy in sent1:
        copy.start()

    def conv_own(src, w, f, b):
        z = dot(src[f, 0:PIX], w[0, b, 0:C])
        z = z + dot(src[f, COLS : COLS + PIX], w[1, b, 0:C])
        return z + dot(src[f, 2 * COLS : 2 * COLS + PIX], w[2, b, 0:C])

    loads[3].wait()
    parts = []
    for b in range(3):
        c0, c1, c2 = [dot(up[...], w1[a, b, C : 2 * C]) for a in range(3)]
        parts.append((c1 + c2, c0 + c1 + c2, c0 + c1))
    for k in range(3):
        cclass[k] = from_west(parts[0][k]) + parts[1][k] + from_east(parts[2][k]) + b1[...]

    def own1(f, _):
        z = from_west(conv_own(xp, w1, f, 0)) + conv_own(xp, w1, f, 1) + from_east(conv_own(xp, w1, f, 2))
        at = pl.ds(pl.multiple_of(f * COLS, COLS), COLS)
        acc[f, 0:COLS] = z[0:COLS] + cclass[0, at]
        for i in range(1, ROWS - 1):
            acc[f, i * COLS : (i + 1) * COLS] = z[i * COLS : (i + 1) * COLS] + cclass[1, at]
        acc[f, PIX - COLS : PIX] = z[PIX - COLS : PIX] + cclass[2, at]
        return 0

    lax.fori_loop(0, FACES, own1, 0)

    def edge_rows(rows):
        tops, ends = [], []
        for f in range(FACES):
            face = g * FACES + f
            top_f = jnp.where(first, ns[face, 0], f)
            top_k = jnp.where(first, 2 * code[face, 0], 0)
            end_f = jnp.where(last, ns[face, 1], f)
            end_k = jnp.where(last, 1 + 2 * code[face, 1], 1)
            tops.append(rows[top_k, top_f])
            ends.append(rows[end_k, end_f])
        return tops, ends

    def add_borders(tops, ends, picked, w, wide):
        for k, (row, a) in enumerate(((tops, 0), (ends, 2))):
            z = []
            for b in range(3):
                y = dot(row[0], w[a, b, 0:C])
                if wide:
                    y = y + dot(row[1], w[a, b, C : 2 * C])
                z.append(y)
            zrow[k] = from_west(z[0]) + z[1] + from_east(z[2])
        for k, b in ((0, 0), (1, 2)):
            v = []
            for a in range(3):
                y = dot(picked[0][48 * k : 48 * k + 48], w[a, b, 0:C])
                if wide:
                    y = y + dot(picked[1][48 * k : 48 * k + 48], w[a, b, C : 2 * C])
                v.append(y)
            zcol[k] = along_rows(*v)

    column = column_of((COLS, C))

    def with_borders(f, i):
        z = acc[f, i * COLS : (i + 1) * COLS]
        if i == 0:
            z = z + zrow[0, pl.ds(pl.multiple_of(f * COLS, COLS), COLS)]
        if i == ROWS - 1:
            z = z + zrow[1, pl.ds(pl.multiple_of(f * COLS, COLS), COLS)]
        west = zcol[0, pl.ds(f * 16 + i + 1, 1), :]
        east = zcol[1, pl.ds(f * 16 + i + 1, 1), :]
        z = z + jnp.where(column == 0, jnp.broadcast_to(west, z.shape), 0.0)
        return z + jnp.where(column == COLS - 1, jnp.broadcast_to(east, z.shape), 0.0)

    for copy in sent1:
        copy.wait_recv()
    picked = dot(pick[...], cols1[...].reshape(groups * BLOCKS * 16, C)).astype(bf16)
    tops, ends = edge_rows(rows1)
    pair = lambda rows: [jnp.concatenate([r[k] for r in rows], axis=0) for k in range(2)]
    add_borders(pair(tops), pair(ends), (picked[0:96], picked[96:192]), w1, True)

    def activate(f, _):
        for i in range(ROWS):
            u = with_borders(f, i)
            h = u / (1.0 + jnp.exp(-u))
            acc[f, i * COLS : (i + 1) * COLS] = h
            hp[f, (i + 1) * COLS : (i + 2) * COLS] = h.astype(bf16)
        return 0

    lax.fori_loop(0, FACES, activate, 0)
    fill_tables(acc, 1.0, cols2, corner2, [])
    for f in range(FACES):
        rows2[2, f] = hp[f, COLS : 2 * COLS]
        rows2[3, f] = hp[f, PIX : PIX + COLS]
    sent2 = copies(1, cols2, corner2, rows2)
    for copy in sent2:
        copy.start()

    loads[4].wait()

    def own2(f, _):
        z = from_west(conv_own(hp, w2, f, 0)) + conv_own(hp, w2, f, 1) + from_east(conv_own(hp, w2, f, 2))
        acc[f] = z + b2[...]
        return 0

    lax.fori_loop(0, FACES, own2, 0)

    for copy in sent2:
        copy.wait_recv()
    picked = dot(pick[0:96, :], cols2[...].reshape(groups * BLOCKS * 16, C)).astype(bf16)
    tops, ends = edge_rows(rows2)
    add_borders(
        [jnp.concatenate(tops, axis=0)], [jnp.concatenate(ends, axis=0)], (picked,), w2, False
    )

    def finish(f, _):
        for i in range(ROWS):
            feature = with_borders(f, i)
            p = pf[f, i * COLS : (i + 1) * COLS]
            denoised = skip_gain * p + output_gain * feature
            out[f, i] = (p + step_ratio * (p - denoised)).astype(bf16)
        return 0

    lax.fori_loop(0, FACES, finish, 0)
    for copy in sent1 + sent2:
        copy.wait_send()


def on_device(groups, tiles, sample, noise, coarse, w1, b1, w2, b2, ns, we, code):
    C = sample.shape[-1]
    hbm = pl.BlockSpec(memory_space=pl.ANY)
    vmem = pl.BlockSpec(memory_space=pltpu.VMEM)
    smem = pl.BlockSpec(memory_space=pltpu.SMEM)
    return pl.pallas_call(
        functools.partial(kernel, groups, tiles),
        out_shape=jax.ShapeDtypeStruct(sample.shape, bf16),
        in_specs=[hbm] * 5 + [vmem] * 2 + [smem] * 3,
        out_specs=vmem,
        scratch_shapes=[
            pltpu.VMEM(sample.shape, bf16),
            pltpu.VMEM(noise.shape, bf16),
            pltpu.VMEM(coarse.shape, bf16),
            pltpu.VMEM(w1.shape, bf16),
            pltpu.VMEM(w2.shape, bf16),
            pltpu.VMEM((FACES, PIX, C), f32),
            pltpu.VMEM((FACES, PIX, C), f32),
            pltpu.VMEM((FACES, PIX + 2 * COLS, C), bf16),
            pltpu.VMEM((FACES, PIX + 2 * COLS, C), bf16),
            pltpu.VMEM((FACES * COLS, C), bf16),
            pltpu.VMEM((3, FACES * COLS, C), f32),
            pltpu.VMEM((groups, BLOCKS, 16, C), bf16),
            pltpu.VMEM((groups, BLOCKS, 16, C), bf16),
            pltpu.VMEM((2, 16, C), bf16),
            pltpu.VMEM((2, 16, C), bf16),
            pltpu.VMEM((4, FACES, 2, COLS, C), bf16),
            pltpu.VMEM((4, FACES, COLS, C), bf16),
            pltpu.VMEM((192, groups * BLOCKS * 16), bf16),
            pltpu.VMEM((2, 48, C), f32),
            pltpu.VMEM((2, FACES * COLS, C), f32),
            pltpu.SemaphoreType.DMA((5,)),
            pltpu.SemaphoreType.DMA((2, 13)),
            pltpu.SemaphoreType.DMA((2, 13)),
        ],
        compiler_params=pltpu.CompilerParams(
            collective_id=0, has_side_effects=True, vmem_limit_bytes=32 * 2**20
        ),
    )(sample, noise, coarse, w1, w2, b1.reshape(1, C), b2.reshape(1, C), ns, we, code)


def solution(mesh):
    return jax.shard_map(
        functools.partial(on_device, mesh.shape["face"], mesh.shape["tile"]),
        mesh=mesh,
        in_specs=(P("face", "tile", None, None),) * 3 + (P(),) * 7,
        out_specs=P("face", "tile", None, None),
        check_vma=False,
    )
```

time: 80.3 us -> 37.9 us (0.47)
  the two profiles are of different devices: /device:TPU:128 before, /device:TPU:1 now
where the time goes in v1:
time: 37.9 us; the launch traced here: 37.7 us
  Pallas kernels  31.9 us (84%)
  local copies, waits for them, and re-layouts  5.71 us (15%)
    pallas_call x1, Pallas kernels, on_device(): pl.pallas_call(functools.partial(kernel, groups, tiles), out_shape=jax.Sh...  31.9 us
    unnamed x17, local copies, waits for them, and re-layouts  5.71 us

profile of v1, /device:TPU:1, one launch (start us, length us, event | category | flops | bytes accessed | tf_op | source)
XLA Modules:
  0.0 37.7 jit_solution(15263996826236602780)
XLA Ops:
  0.0 0.0 copy-start.5
  0.0 0.0 copy-start
  0.0 0.0 copy-start.4
  0.0 0.0 copy-start.3
  0.0 0.0 copy-start.2
  0.0 0.0 copy-start.1
  0.0 0.9 %copy.12.ns = s32[12,2]{1,0:T(8,128)S(1)} copy(s32[12,2]{0,1:T(2,128)} %param.17) | data formatting | bytes 192 | tf_op args[7]
  0.9 0.8 %copy.13.we = s32[12,2]{1,0:T(8,128)S(1)} copy(s32[12,2]{0,1:T(2,128)} %param.18) | data formatting | bytes 192 | tf_op args[8]
  1.7 0.8 %copy.14.code = s32[12,4]{1,0:T(8,128)S(1)} copy(s32[12,4]{0,1:T(4,128)} %param.19) | data formatting | bytes 384 | tf_op args[9]
  2.5 2.5 %copy.11.w1_hbm = bf16[3,3,384,192]{3,2,1,0:T(8,128)(2,1)S(1)} copy(bf16[3,3,384,192]{2,3,1,0:T(8,128)(2,1)} %param.13) | data formatting | bytes 2654208 | tf_op args[3]
  5.0 0.0 copy-done.5
  5.0 0.0 copy-done
  5.0 0.0 copy-done.4
  5.0 0.0 copy-done.3
  5.0 0.0 copy-done.2
  5.0 0.0 copy-done.1
  5.1 31.9 %shard_map.100 = bf16[3,8,32,192]{3,2,1,0:T(8,128)(2,1)S(1)} custom-call(bf16[3,8,32,192]{3,2,1,0:T(8,128)(2,1)S(1)} %copy-done.1, bf16[3,8,32,192]{3,2,1,0:T(8,128)(2,1)S(1)} %copy-done.2, bf16[3,1,4,192]{3,2,1,0:T(4,128)(2,1)S(1)} %copy-done.3, bf16[3,3,384,192]{3,2,1,0:T(8,128)(2,1)S(1)} %copy.11.w1_hbm, bf16[3,3,192,192]{3,2,1,0:T(8,128)(2,1)S(1)} %copy-done, ...), custom_call_target="tpu_custom_call" | custom-call | tf_op jit(solution)/shard_map/pallas_call | solution.py:348
  37.0 0.7 %copy.16 = bf16[3,8,32,192]{3,2,1,0:T(8,128)(2,1)} copy(bf16[3,8,32,192]{3,2,1,0:T(8,128)(2,1)S(1)} %shard_map.100) | data formatting | bytes 589824
Async XLA Ops:
  0.0 5.0 %copy-start.5 = (f32[192]{0:T(256)S(1)}, f32[192]{0:T(256)}, u32[]{:S(2)}) copy-start(f32[192]{0:T(256)} %param.16) | copy-start | bytes 2308
  0.0 5.0 %copy-start = (bf16[3,3,192,192]{3,2,1,0:T(8,128)(2,1)S(1)}, bf16[3,3,192,192]{3,2,1,0:T(8,128)(2,1)}, u32[]{:S(2)}) copy-start(bf16[3,3,192,192]{3,2,1,0:T(8,128)(2,1)} %w2_hbm.1) | copy-start | bytes 1990660
  0.0 5.0 %copy-start.4 = (f32[192]{0:T(256)S(1)}, f32[192]{0:T(256)}, u32[]{:S(2)}) copy-start(f32[192]{0:T(256)} %param.14) | copy-start | bytes 2308
  0.0 5.0 %copy-start.3 = (bf16[3,1,4,192]{3,2,1,0:T(4,128)(2,1)S(1)}, bf16[3,1,4,192]{3,2,1,0:T(4,128)(2,1)}, u32[]{:S(2)}) copy-start(bf16[3,1,4,192]{3,2,1,0:T(4,128)(2,1)} %coarse_hbm.1) | copy-start | bytes 13828
  0.0 5.0 %copy-start.2 = (bf16[3,8,32,192]{3,2,1,0:T(8,128)(2,1)S(1)}, bf16[3,8,32,192]{3,2,1,0:T(8,128)(2,1)}, u32[]{:S(2)}) copy-start(bf16[3,8,32,192]{3,2,1,0:T(8,128)(2,1)} %noise_hbm.1) | copy-start | bytes 884740
  0.0 5.0 %copy-start.1 = (bf16[3,8,32,192]{3,2,1,0:T(8,128)(2,1)S(1)}, bf16[3,8,32,192]{3,2,1,0:T(8,128)(2,1)}, u32[]{:S(2)}) copy-start(bf16[3,8,32,192]{3,2,1,0:T(8,128)(2,1)} %sample_hbm.1) | copy-start | bytes 884740

commit v2 on v1

v2 whole, which is shorter than its diff:
```python
import functools

import jax
import jax.numpy as jnp
from jax import lax
from jax.experimental import pallas as pl
from jax.experimental.pallas import tpu as pltpu
from jax.sharding import PartitionSpec as P

MESH = pl.DeviceIdType.MESH
f32 = jnp.float32
bf16 = jnp.bfloat16
i32 = jnp.int32

noise_gain = 0.6
input_gain = 0.7071067811865476
skip_gain = 0.5
output_gain = 0.7071067811865476
step_ratio = -0.4

UP = 8
FACES = 3
ROWS = 8
COLS = 32
COARSE = COLS // UP
PIX = ROWS * COLS
SIDES = 2 * FACES
WIDE = 256

BLOCKS = 12
OUTER, INNER, OVER, UNDER, EMPTY = 1, 4, 7, 9, 11
STACK = 16
FIRST = 4


def dot(a, b):
    return jnp.dot(a, b, preferred_element_type=f32)


def dot_t(a, b):
    return lax.dot_general(a, b, (((1,), (1,)), ((), ())), preferred_element_type=f32)


def column_of(shape):
    return lax.rem(lax.broadcasted_iota(i32, shape, 0), COLS)


def from_west(z):
    return jnp.where(column_of(z.shape) == 0, 0.0, pltpu.roll(z, 1, 0))


def from_east(z):
    return jnp.where(column_of(z.shape) == COLS - 1, 0.0, pltpu.roll(z, z.shape[0] - 1, 0))


def along_rows(v0, v1, v2):
    return pltpu.roll(v0, 1, 0) + v1 + pltpu.roll(v2, v2.shape[0] - 1, 0)


def silu(u):
    return u / (1.0 + jnp.exp(-u))


def spread(rows, count):
    width = rows[0][1].shape[1]
    place = lax.broadcasted_iota(i32, (count, width), 0)
    out = jnp.zeros((count, width), f32)
    for at, row in rows:
        out = jnp.where(place == at, jnp.broadcast_to(row, (count, width)), out)
    return out


def kernel(
    groups,
    tiles,
    sample_hbm,
    noise_hbm,
    coarse_hbm,
    ns_hbm,
    we_hbm,
    code_hbm,
    w1_hbm,
    b1_hbm,
    w2_hbm,
    b2_hbm,
    out,
    sample,
    noise,
    coarse,
    ns,
    we,
    code,
    w1,
    b1,
    w2,
    b2,
    pf,
    acc,
    xp,
    hp,
    up,
    cclass,
    cols,
    corner,
    rows1,
    rows2,
    pick,
    zcol,
    zrow,
    load_sem,
    send_sem,
    recv_sem,
):
    g = lax.axis_index("face")
    t = lax.axis_index("tile")
    above = lax.rem(t + tiles - 1, tiles)
    below = lax.rem(t + 1, tiles)
    first = t == 0
    last = t == tiles - 1
    C = acc.shape[2]
    lines = groups * BLOCKS * 16

    loads = [
        pltpu.make_async_copy(src, dst, load_sem.at[i])
        for i, (src, dst) in enumerate(
            [
                (sample_hbm, sample),
                (noise_hbm, noise),
                (coarse_hbm, coarse),
                (ns_hbm, ns),
                (we_hbm, we),
                (code_hbm, code),
                (w1_hbm, w1),
                (b1_hbm, b1),
                (w2_hbm, w2),
                (b2_hbm, b2),
            ]
        )
    ]
    for copy in loads[:6]:
        copy.start()

    barrier = pltpu.get_barrier_semaphore()
    for d in (2, 1, 3, 0):
        for k, there in enumerate((t, above, below)):
            if d or k:
                pl.semaphore_signal(
                    barrier, inc=1, device_id=(lax.rem(g + d, groups), there), device_id_type=MESH
                )

    for f in range(FACES):
        zero_row = jnp.zeros((COLS, WIDE), bf16)
        xp[f, 0:COLS] = zero_row
        xp[f, COLS + PIX : 2 * COLS + PIX] = zero_row
        xp[f, COLS : COLS + PIX, 128:WIDE] = jnp.zeros((PIX, WIDE - 128), bf16)
        pf[f, :, 128:WIDE] = jnp.zeros((PIX, WIDE - 128), f32)
    for d in range(groups):
        cols[d, EMPTY] = jnp.zeros((16, WIDE), bf16)

    for copy in loads[:3]:
        copy.wait()
    for f in range(FACES):
        p = sample[f].astype(f32) + noise_gain * noise[f].astype(f32)
        p = p.reshape(PIX, C)
        pf[f, :, 0:C] = p
        xp[f, COLS : COLS + PIX, 0:C] = (p * input_gain).astype(bf16)
        for r in range(2):
            rows1[2, f, r] = xp[f, (1 + r) * COLS : (2 + r) * COLS]
            rows1[3, f, r] = xp[f, PIX - COLS + r * COLS : PIX + r * COLS]
    raw, tops, ends = [], [], []
    for f in range(FACES):
        c = coarse[f, 0].astype(f32)
        c = jnp.concatenate([jnp.zeros((COARSE, WIDE - C), f32), c], axis=1)
        each = [c[j : j + 1] for j in range(COARSE)]
        raw += [(4 * f + j, each[j]) for j in range(COARSE)]
        edges = [(24 + 2 * f, each[0]), (25 + 2 * f, each[COARSE - 1])]
        wide = jnp.concatenate([jnp.broadcast_to(e, (UP, WIDE)) for e in each], axis=0).astype(bf16)
        up[f * COLS : (f + 1) * COLS] = wide
        rows1[2, f, 2] = wide
        rows1[3, f, 2] = wide
        tops += edges
        ends += edges
        for k, block, j in ((0, OUTER, 0), (3, OUTER, COLS - 1), (1, INNER, 1), (2, INNER, COLS - 2)):
            line = [pf[f, i * COLS + j : i * COLS + j + 1, :] * input_gain for i in range(ROWS)]
            half = spread(list(enumerate(line)), ROWS)
            if k in (0, 1):
                lower = half
            else:
                cols[g, block + f] = jnp.concatenate([lower, half], axis=0).astype(bf16)
            tops += [(8 * f + 2 * k + r, line[r]) for r in range(2)]
            ends += [(8 * f + 2 * k + r, line[ROWS - 2 + r]) for r in range(2)]
    cols[g, 0] = spread(raw, 16).astype(bf16)
    corner[0] = spread(tops, 32).astype(bf16).reshape(2, 16, WIDE)
    corner[1] = spread(ends, 32).astype(bf16).reshape(2, 16, WIDE)

    sent = []

    def add(src, dst, there):
        n = len(sent)
        sent.append(
            pltpu.make_async_remote_copy(
                src_ref=src,
                dst_ref=dst,
                send_sem=send_sem.at[n],
                recv_sem=recv_sem.at[n],
                device_id=there,
                device_id_type=MESH,
            )
        )

    table = cols.at[g, pl.ds(0, OVER)]
    over = cols.at[g, pl.ds(OVER, 2)]
    under = cols.at[g, pl.ds(UNDER, 2)]
    for d in (2, 1, 3):
        far = lax.rem(g + d, groups)
        add(corner.at[0], under, (far, above))
        add(corner.at[1], over, (far, below))
        add(table, table, (far, t))
    add(corner.at[0], under, (g, above))
    add(corner.at[1], over, (g, below))
    add(rows1.at[2], rows1.at[1], (g, above))
    add(rows1.at[3], rows1.at[0], (g, below))

    pl.semaphore_wait(barrier, 3 * groups - 1)
    for copy in sent:
        copy.start()
    for copy in loads[6:]:
        copy.start()
    for copy in loads[3:6]:
        copy.wait()

    lane = lax.broadcasted_iota(i32, (STACK, lines), 1)
    place = lax.broadcasted_iota(i32, (STACK, lines), 0)

    def split(face):
        group = sum((face >= FACES * k).astype(i32) for k in range(1, groups))
        return group, face - FACES * group

    def across(face, side):
        edge = code[2 + side, face]
        return we[side, face], 3 * jnp.where(side == 1, edge, 1 - edge)

    def write_pick(at, face, column, beyond):
        group, f = split(face)
        base = group * (BLOCKS * 16)
        inner = ((column == 1) | (column == 2)).astype(i32)
        high = (column >= 2).astype(i32)

        def line(ff, row):
            if row < 0:
                return base + OVER * 16 + ff * 8 + column * 2 + 2 + row
            if row >= ROWS:
                return base + UNDER * 16 + ff * 8 + column * 2 + row - ROWS
            return base + (OUTER + inner * (INNER - OUTER) + ff) * 16 + high * 8 + row

        def condition(ff, row):
            if row < 0:
                return base + OVER * 16 + 24 + ff * 2 + high
            if row >= ROWS:
                return base + UNDER * 16 + 24 + ff * 2 + high
            return base + ff * COARSE + high * (COARSE - 1)

        n, s = ns[0, face], ns[1, face]
        flip_n, flip_s = code[0, face] == 1, code[1, face] == 1
        for part, where in enumerate((line, condition)):
            north = jnp.where(beyond, -1, jnp.where(flip_n, where(n, 0), where(n, -1)))
            south = jnp.where(beyond, -1, jnp.where(flip_s, where(s, ROWS - 1), where(s, ROWS)))
            target = jnp.broadcast_to(where(f, 0), place.shape)
            if part == 0:
                target = target + place - FIRST
            for q, value in (
                (0, where(f, -2)),
                (1, where(f, -1)),
                (2, jnp.where(first, -1, where(f, 0))),
                (3, jnp.where(first, north, where(f, -1))),
                (12, jnp.where(last, south, where(f, ROWS))),
                (13, jnp.where(last, -1, where(f, ROWS - 1))),
                (14, where(f, ROWS)),
                (15, where(f, ROWS + 1)),
            ):
                target = jnp.where(place == q, value, target)
            at = pl.multiple_of(at, STACK)
            pick[part, pl.ds(at, STACK), :] = jnp.where(lane == target, 1.0, 0.0).astype(bf16)

    def pick_side(n, _):
        side = (n >= FACES).astype(i32)
        face = g * FACES + n - FACES * side
        near, column = across(face, side)
        west_face, west_column = across(near, 0)
        east_face, east_column = across(near, 1)
        at_west = column == 0
        at_east = column == 3
        write_pick(n * STACK, near, column, True)
        write_pick(
            (SIDES + n) * STACK,
            jnp.where(at_west, west_face, near),
            jnp.where(at_west, west_column, 2),
            at_west,
        )
        write_pick((2 * SIDES + n) * STACK, near, column, False)
        write_pick(
            (3 * SIDES + n) * STACK,
            jnp.where(at_east, east_face, near),
            jnp.where(at_east, east_column, 1),
            at_east,
        )
        return 0

    lax.fori_loop(0, SIDES, pick_side, 0)

    def tap1(x, a, b):
        return dot_t(x, w1[a, b, :, 0:WIDE])

    def tap1_coarse(x, a, b):
        return dot_t(x, w1[a, b, :, w1.shape[3] - WIDE :])

    def tap2(x, a, b):
        return dot(x, w2[a, b])

    def conv_own(src, tap, f, b):
        z = tap(src[f, 0:PIX], 0, b)
        z = z + tap(src[f, COLS : COLS + PIX], 1, b)
        return z + tap(src[f, 2 * COLS : 2 * COLS + PIX], 2, b)

    for copy in loads[6:]:
        copy.wait()
    parts = []
    for b in range(3):
        c0, c1, c2 = [tap1_coarse(up[...], a, b) for a in range(3)]
        parts.append((c1 + c2, c0 + c1 + c2, c0 + c1))
    for k in range(3):
        cclass[k] = from_west(parts[0][k]) + parts[1][k] + from_east(parts[2][k]) + b1[...]

    def own1(f, _):
        z = from_west(conv_own(xp, tap1, f, 0)) + conv_own(xp, tap1, f, 1) + from_east(conv_own(xp, tap1, f, 2))
        at = pl.ds(pl.multiple_of(f * COLS, COLS), COLS)
        for i in range(ROWS):
            k = 0 if i == 0 else 2 if i == ROWS - 1 else 1
            acc[f, i * COLS : (i + 1) * COLS] = z[i * COLS : (i + 1) * COLS] + cclass[k, at]
        return 0

    lax.fori_loop(0, FACES, own1, 0)

    for copy in sent:
        copy.wait_recv()
    table = cols[...].reshape(lines, WIDE)
    picked = [dot(pick[part], table).astype(bf16) for part in range(2)]

    tops, ends, after, before = [], [], [], []
    for f in range(FACES):
        face = g * FACES + f
        n, s = jnp.where(first, ns[0, face], f), jnp.where(last, ns[1, face], f)
        flip_n, flip_s = code[0, face], code[1, face]
        k = jnp.where(first, 2 * flip_n, 0)
        r = jnp.where(k == 0, 1, 0)
        tops.append((rows1[k, n, r], rows1[k, n, 2]))
        k = jnp.where(last, 1 + 2 * flip_s, 1)
        r = jnp.where(k == 1, 0, 1)
        ends.append((rows1[k, s, r], rows1[k, s, 2]))
        s = jnp.where(first, ns[1, face], f)
        k = jnp.where(first, 2 - 2 * flip_s, 2)
        r = jnp.where(k == 0, 1, 0)
        after.append((rows1[k, s, r], rows1[k, s, 2]))
        n = jnp.where(last, ns[0, face], f)
        k = jnp.where(last, 3 - 2 * flip_n, 3)
        r = jnp.where(k == 1, 0, 1)
        before.append((rows1[k, n, r], rows1[k, n, 2]))

    def landed(k, r):
        return [(rows1[k, f, r], rows1[k, f, 2]) for f in range(FACES)]

    ROW = FACES * COLS
    stacks = (
        landed(0, 0) + tops + before,
        landed(0, 1) + landed(1, 0),
        after + landed(1, 1) + ends,
    )
    half = FACES * STACK
    sides = SIDES * STACK
    z_over, z_under, z_top, z_end = [], [], [], []
    v_side, v_near = [[], []], []
    for b in range(3):
        over, under, near = 0.0, 0.0, []
        for a in range(3):
            y = 0.0
            for part, tap in enumerate((tap1, tap1_coarse)):
                chosen = picked[part]
                if b == 0:
                    extra = [chosen[0:half], chosen[sides : 2 * sides]]
                elif b == 1:
                    extra = [chosen[2 * sides : 3 * sides]]
                else:
                    extra = [chosen[half : 2 * half], chosen[3 * sides : 4 * sides]]
                y = y + tap(jnp.concatenate([r[part] for r in stacks[a]] + extra, axis=0), a, b)
            if a == 0:
                over = over + y[0:ROW]
                z_top.append(y[ROW : 2 * ROW])
                under = under + y[2 * ROW : 3 * ROW]
            elif a == 1:
                over = over + y[0:ROW]
                under = under + y[ROW : 2 * ROW]
            else:
                over = over + y[0:ROW]
                under = under + y[ROW : 2 * ROW]
                z_end.append(y[2 * ROW : 3 * ROW])
            rest = y[len(stacks[a]) * COLS :]
            if b != 1:
                v_side[b // 2].append(rest[0:half])
                rest = rest[half:]
            near.append(rest)
        z_over.append(over)
        z_under.append(under)
        v_near.append(near)

    for k, z in enumerate((z_over, z_under, z_top, z_end)):
        z = from_west(z[0]) + z[1] + from_east(z[2])
        zrow[k] = z if k >= 2 else z + b1[...]
    for k in range(2):
        zcol[k] = along_rows(*v_side[k])
    near = along_rows(*[v_near[0][a] + v_near[1][a] + v_near[2][a] for a in range(3)]) + b1[...]
    near = silu(near)
    place = lax.rem(lax.broadcasted_iota(i32, near.shape, 0), STACK)
    low = jnp.where(first, 0.0, pltpu.roll(near, 2, 0))
    high = jnp.where(last, 0.0, pltpu.roll(near, near.shape[0] - 2, 0))
    near = jnp.where(place == FIRST - 1, low, jnp.where(place == FIRST + ROWS, high, near))
    near = near.astype(bf16)

    column = column_of((COLS, C))

    def with_sides(z, f, q):
        west = zcol[0, pl.ds(f * STACK + q, 1), :]
        east = zcol[1, pl.ds(f * STACK + q, 1), :]
        z = z + jnp.where(column == 0, jnp.broadcast_to(west, z.shape), 0.0)
        return z + jnp.where(column == COLS - 1, jnp.broadcast_to(east, z.shape), 0.0)

    def activate(f, _):
        at = pl.ds(pl.multiple_of(f * COLS, COLS), COLS)
        rows2[0, f] = silu(with_sides(zrow[0, at], f, 1)).astype(bf16)
        rows2[1, f] = silu(with_sides(zrow[1, at], f, STACK - 2)).astype(bf16)
        for i in range(ROWS):
            z = acc[f, i * COLS : (i + 1) * COLS]
            if i == 0:
                z = z + zrow[2, at]
            if i == ROWS - 1:
                z = z + zrow[3, at]
            h = silu(with_sides(z, f, FIRST + i)).astype(bf16)
            hp[f, (i + 1) * COLS : (i + 2) * COLS] = h
            if i == 0:
                rows2[2, f] = h
            if i == ROWS - 1:
                rows2[3, f] = h
        return 0

    lax.fori_loop(0, FACES, activate, 0)
    for f in range(FACES):
        face = g * FACES + f
        n, s = jnp.where(first, ns[0, face], f), jnp.where(last, ns[1, face], f)
        hp[f, 0:COLS] = rows2[jnp.where(first, 2 * code[0, face], 0), n]
        hp[f, PIX + COLS : PIX + 2 * COLS] = rows2[jnp.where(last, 1 + 2 * code[1, face], 1), s]
    for k in range(2):
        zcol[k] = along_rows(*[tap2(near[half * k : half * k + half], a, 2 * k) for a in range(3)])

    def finish(f, _):
        z = from_west(conv_own(hp, tap2, f, 0)) + conv_own(hp, tap2, f, 1) + from_east(conv_own(hp, tap2, f, 2))
        for i in range(ROWS):
            feature = with_sides(z[i * COLS : (i + 1) * COLS], f, FIRST + i) + b2[...]
            p = pf[f, i * COLS : (i + 1) * COLS, 0:C]
            denoised = skip_gain * p + output_gain * feature
            out[f, i] = (p + step_ratio * (p - denoised)).astype(bf16)
        return 0

    lax.fori_loop(0, FACES, finish, 0)
    for copy in sent:
        copy.wait_send()


def on_device(groups, tiles, sample, noise, coarse, w1, b1, w2, b2, ns, we, code):
    C = sample.shape[-1]
    w1 = jnp.swapaxes(w1, 2, 3)
    operands = (sample, noise, coarse, ns.T, we.T, code.T, w1, b1.reshape(1, C), w2, b2.reshape(1, C))
    return pl.pallas_call(
        functools.partial(kernel, groups, tiles),
        out_shape=jax.ShapeDtypeStruct(sample.shape, bf16),
        in_specs=[pl.BlockSpec(memory_space=pltpu.HBM)] * len(operands),
        out_specs=pl.BlockSpec(memory_space=pltpu.VMEM),
        scratch_shapes=[
            (pltpu.SMEM if x.dtype == i32 else pltpu.VMEM)(x.shape, x.dtype) for x in operands
        ]
        + [
            pltpu.VMEM((FACES, PIX, WIDE), f32),
            pltpu.VMEM((FACES, PIX, C), f32),
            pltpu.VMEM((FACES, PIX + 2 * COLS, WIDE), bf16),
            pltpu.VMEM((FACES, PIX + 2 * COLS, C), bf16),
            pltpu.VMEM((FACES * COLS, WIDE), bf16),
            pltpu.VMEM((3, FACES * COLS, C), f32),
            pltpu.VMEM((groups, BLOCKS, 16, WIDE), bf16),
            pltpu.VMEM((2, 2, 16, WIDE), bf16),
            pltpu.VMEM((4, FACES, 3, COLS, WIDE), bf16),
            pltpu.VMEM((4, FACES, COLS, C), bf16),
            pltpu.VMEM((2, 4 * SIDES * STACK, groups * BLOCKS * 16), bf16),
            pltpu.VMEM((2, FACES * STACK, C), f32),
            pltpu.VMEM((4, FACES * COLS, C), f32),
            pltpu.SemaphoreType.DMA((len(operands),)),
            pltpu.SemaphoreType.DMA((13,)),
            pltpu.SemaphoreType.DMA((13,)),
        ],
        compiler_params=pltpu.CompilerParams(
            collective_id=0, has_side_effects=True, vmem_limit_bytes=32 * 2**20
        ),
    )(*operands)


def solution(mesh):
    return jax.shard_map(
        functools.partial(on_device, mesh.shape["face"], mesh.shape["tile"]),
        mesh=mesh,
        in_specs=(P("face", "tile", None, None),) * 3 + (P(),) * 7,
        out_specs=P("face", "tile", None, None),
        check_vma=False,
    )
```

time: 37.9 us -> 36.7 us (0.968)
  Pallas kernels: 31.9 us -> 27 us
  local copies, waits for them, and re-layouts: 5.71 us -> 9.31 us
    pallas_call x1, Pallas kernels: 31.9 us -> 27 us  [on_device(): pl.pallas_call(functools.partial(kernel, groups, tiles), out_shape=jax.Sh...]
    unnamed x17 -> x21, local copies, waits for them, and re-layouts: 5.71 us -> 9.31 us
where the time goes in v2:
time: 36.7 us; the launch traced here: 36.3 us
  Pallas kernels  27 us (74%)
  local copies, waits for them, and re-layouts  9.31 us (25%)
    pallas_call x1, Pallas kernels, on_device(): pl.pallas_call(functools.partial(kernel, groups, tiles), out_shape=jax.Sh...  27 us
    unnamed x21, local copies, waits for them, and re-layouts  9.31 us

profile of v2, /device:TPU:1, one launch (start us, length us, event | category | flops | bytes accessed | tf_op | source)
XLA Modules:
  0.0 36.3 jit_solution(13070313606359174994)
XLA Ops:
  0.0 0.0 copy-start
  0.0 1.3 %copy-done = bf16[3,3,384,192]{2,3,1,0:T(8,128)(2,1)S(1)} copy-done((bf16[3,3,384,192]{2,3,1,0:T(8,128)(2,1)S(1)}, bf16[3,3,384,192]{2,3,1,0:T(8,128)(2,1)}, u32[]{:S(2)}) %copy-start) | copy-done | bytes 1327128
  1.3 0.0 copy-start.1
  1.3 1.2 %copy-done.1 = bf16[3,3,192,192]{3,2,1,0:T(8,128)(2,1)S(1)} copy-done((bf16[3,3,192,192]{3,2,1,0:T(8,128)(2,1)S(1)}, bf16[3,3,192,192]{3,2,1,0:T(8,128)(2,1)}, u32[]{:S(2)}) %copy-start.1) | copy-done | bytes 663576
  2.5 0.0 copy-start.2
  2.5 1.0 %copy-done.2 = bf16[3,8,32,192]{3,2,1,0:T(8,128)(2,1)S(1)} copy-done((bf16[3,8,32,192]{3,2,1,0:T(8,128)(2,1)S(1)}, bf16[3,8,32,192]{3,2,1,0:T(8,128)(2,1)}, u32[]{:S(2)}) %copy-start.2) | copy-done | bytes 294936
  3.5 0.0 copy-start.3
  3.5 1.0 %copy-done.3 = bf16[3,8,32,192]{3,2,1,0:T(8,128)(2,1)S(1)} copy-done((bf16[3,8,32,192]{3,2,1,0:T(8,128)(2,1)S(1)}, bf16[3,8,32,192]{3,2,1,0:T(8,128)(2,1)}, u32[]{:S(2)}) %copy-start.3) | copy-done | bytes 294936
  4.5 0.0 copy-start.4
  4.5 0.7 %copy-done.4 = bf16[3,1,4,192]{3,2,1,0:T(4,128)(2,1)S(1)} copy-done((bf16[3,1,4,192]{3,2,1,0:T(4,128)(2,1)S(1)}, bf16[3,1,4,192]{3,2,1,0:T(4,128)(2,1)}, u32[]{:S(2)}) %copy-start.4) | copy-done | bytes 4632
  5.2 0.0 copy-start.5
  5.2 0.7 %copy-done.5 = s32[12,4]{0,1:T(4,128)S(1)} copy-done((s32[12,4]{0,1:T(4,128)S(1)}, s32[12,4]{0,1:T(4,128)}, u32[]{:S(2)}) %copy-start.5) | copy-done | bytes 216
  5.9 0.0 copy-start.6
  5.9 0.7 %copy-done.6 = s32[12,2]{0,1:T(2,128)S(1)} copy-done((s32[12,2]{0,1:T(2,128)S(1)}, s32[12,2]{0,1:T(2,128)}, u32[]{:S(2)}) %copy-start.6) | copy-done | bytes 120
  6.5 0.0 copy-start.7
  6.5 0.7 %copy-done.7 = s32[12,2]{0,1:T(2,128)S(1)} copy-done((s32[12,2]{0,1:T(2,128)S(1)}, s32[12,2]{0,1:T(2,128)}, u32[]{:S(2)}) %copy-start.7) | copy-done | bytes 120
  7.2 0.0 copy-start.8
  7.2 0.7 %copy-done.8 = f32[192]{0:T(256)S(1)} copy-done((f32[192]{0:T(256)S(1)}, f32[192]{0:T(256)}, u32[]{:S(2)}) %copy-start.8) | copy-done | bytes 792
  7.9 0.0 copy-start.9
  7.9 0.7 %copy-done.9 = f32[192]{0:T(256)S(1)} copy-done((f32[192]{0:T(256)S(1)}, f32[192]{0:T(256)}, u32[]{:S(2)}) %copy-start.9) | copy-done | bytes 792
  8.6 27.0 %shard_map.100 = bf16[3,8,32,192]{3,2,1,0:T(8,128)(2,1)S(1)} custom-call(bf16[3,8,32,192]{3,2,1,0:T(8,128)(2,1)S(1)} %copy-done.2, bf16[3,8,32,192]{3,2,1,0:T(8,128)(2,1)S(1)} %copy-done.3, bf16[3,1,4,192]{3,2,1,0:T(4,128)(2,1)S(1)} %copy-done.4, s32[2,12]{1,0:T(2,128)S(1)} %bitcast.8, s32[2,12]{1,0:T(2,128)S(1)} %bitcast.9, s32[4,12]{1,0:T(4,128)S(1)} %bitcast.7, ...), custom_call_target="tpu_custom_call" | custom-call | tf_op jit(solution)/shard_map/pallas_call | solution.py:481
  35.5 0.7 %copy.12 = bf16[3,8,32,192]{3,2,1,0:T(8,128)(2,1)} copy(bf16[3,8,32,192]{3,2,1,0:T(8,128)(2,1)S(1)} %shard_map.100) | data formatting | bytes 589824
Async XLA Ops:
  0.0 1.3 %copy-start = (bf16[3,3,384,192]{2,3,1,0:T(8,128)(2,1)S(1)}, bf16[3,3,384,192]{2,3,1,0:T(8,128)(2,1)}, u32[]{:S(2)}) copy-start(bf16[3,3,384,192]{2,3,1,0:T(8,128)(2,1)} %param.13) | copy-start | bytes 3981316
  1.3 1.2 %copy-start.1 = (bf16[3,3,192,192]{3,2,1,0:T(8,128)(2,1)S(1)}, bf16[3,3,192,192]{3,2,1,0:T(8,128)(2,1)}, u32[]{:S(2)}) copy-start(bf16[3,3,192,192]{3,2,1,0:T(8,128)(2,1)} %w2_hbm.1) | copy-start | bytes 1990660
  2.5 1.0 %copy-start.2 = (bf16[3,8,32,192]{3,2,1,0:T(8,128)(2,1)S(1)}, bf16[3,8,32,192]{3,2,1,0:T(8,128)(2,1)}, u32[]{:S(2)}) copy-start(bf16[3,8,32,192]{3,2,1,0:T(8,128)(2,1)} %sample_hbm.1) | copy-start | bytes 884740
  3.5 1.0 %copy-start.3 = (bf16[3,8,32,192]{3,2,1,0:T(8,128)(2,1)S(1)}, bf16[3,8,32,192]{3,2,1,0:T(8,128)(2,1)}, u32[]{:S(2)}) copy-start(bf16[3,8,32,192]{3,2,1,0:T(8,128)(2,1)} %noise_hbm.1) | copy-start | bytes 884740
  4.5 0.7 %copy-start.4 = (bf16[3,1,4,192]{3,2,1,0:T(4,128)(2,1)S(1)}, bf16[3,1,4,192]{3,2,1,0:T(4,128)(2,1)}, u32[]{:S(2)}) copy-start(bf16[3,1,4,192]{3,2,1,0:T(4,128)(2,1)} %coarse_hbm.1) | copy-start | bytes 13828
  5.2 0.7 %copy-start.5 = (s32[12,4]{0,1:T(4,128)S(1)}, s32[12,4]{0,1:T(4,128)}, u32[]{:S(2)}) copy-start(s32[12,4]{0,1:T(4,128)} %param.19) | copy-start | bytes 580
  5.9 0.7 %copy-start.6 = (s32[12,2]{0,1:T(2,128)S(1)}, s32[12,2]{0,1:T(2,128)}, u32[]{:S(2)}) copy-start(s32[12,2]{0,1:T(2,128)} %param.17) | copy-start | bytes 292
  6.5 0.7 %copy-start.7 = (s32[12,2]{0,1:T(2,128)S(1)}, s32[12,2]{0,1:T(2,128)}, u32[]{:S(2)}) copy-start(s32[12,2]{0,1:T(2,128)} %param.18) | copy-start | bytes 292
  7.2 0.7 %copy-start.8 = (f32[192]{0:T(256)S(1)}, f32[192]{0:T(256)}, u32[]{:S(2)}) copy-start(f32[192]{0:T(256)} %param.14) | copy-start | bytes 2308
  7.9 0.7 %copy-start.9 = (f32[192]{0:T(256)S(1)}, f32[192]{0:T(256)}, u32[]{:S(2)}) copy-start(f32[192]{0:T(256)} %param.16) | copy-start | bytes 2308

commit v3 on v2

--- a/solution.py
+++ b/solution.py
@@ -507,7 +507,7 @@
         compiler_params=pltpu.CompilerParams(
             collective_id=0, has_side_effects=True, vmem_limit_bytes=32 * 2**20
         ),
-    )(*operands)
+    )(*[pltpu.with_memory_space_constraint(x, pltpu.HBM) for x in operands])
 
 
 def solution(mesh):

time: 36.7 us -> 27.5 us (0.75)
  local copies, waits for them, and re-layouts: 9.31 us -> 0.75 us
  Pallas kernels: 27 us -> 26.6 us
    unnamed x21 -> x1, local copies, waits for them, and re-layouts: 9.31 us -> 0.75 us
    pallas_call x1, Pallas kernels: 27 us -> 26.6 us  [on_device(): pl.pallas_call(functools.partial(kernel, groups, tiles), out_shape=jax.Sh...]
where the time goes in v3:
time: 27.5 us; the launch traced here: 27.3 us
  Pallas kernels  26.6 us (97%)
  local copies, waits for them, and re-layouts  0.75 us (3%)
    pallas_call x1, Pallas kernels, on_device(): pl.pallas_call(functools.partial(kernel, groups, tiles), out_shape=jax.Sh...  26.6 us
    unnamed x1, local copies, waits for them, and re-layouts  0.75 us

profile of v3, /device:TPU:1, one launch (start us, length us, event | category | flops | bytes accessed | tf_op | source)
XLA Modules:
  0.0 27.3 jit_solution(15927799733245893375)
XLA Ops:
  0.0 26.6 %shard_map.100 = bf16[3,8,32,192]{3,2,1,0:T(8,128)(2,1)S(1)} custom-call(bf16[3,8,32,192]{3,2,1,0:T(8,128)(2,1)} %sample_hbm.1, bf16[3,8,32,192]{3,2,1,0:T(8,128)(2,1)} %noise_hbm.1, bf16[3,1,4,192]{3,2,1,0:T(4,128)(2,1)} %coarse_hbm.1, s32[2,12]{1,0:T(2,128)} %bitcast.8, s32[2,12]{1,0:T(2,128)} %bitcast.9, s32[4,12]{1,0:T(4,128)} %bitcast.7, ...), custom_call_target="tpu_custom_call" | custom-call | tf_op jit(solution)/shard_map/pallas_call | solution.py:481
  26.6 0.7 %copy.12 = bf16[3,8,32,192]{3,2,1,0:T(8,128)(2,1)} copy(bf16[3,8,32,192]{3,2,1,0:T(8,128)(2,1)S(1)} %shard_map.100) | data formatting | bytes 589824

commit v4 on v3

--- a/solution.py
+++ b/solution.py
@@ -96,6 +96,9 @@
     b2,
     pf,
     acc,
+    acc2,
+    own_line,
+    z_line,
     xp,
     hp,
     up,
@@ -154,6 +157,8 @@
         xp[f, COLS + PIX : 2 * COLS + PIX] = zero_row
         xp[f, COLS : COLS + PIX, 128:WIDE] = jnp.zeros((PIX, WIDE - 128), bf16)
         pf[f, :, 128:WIDE] = jnp.zeros((PIX, WIDE - 128), f32)
+        hp[f, 0 : 2 * COLS] = jnp.zeros((2 * COLS, C), bf16)
+        hp[f, PIX : PIX + 2 * COLS] = jnp.zeros((2 * COLS, C), bf16)
     for d in range(groups):
         cols[d, EMPTY] = jnp.zeros((16, WIDE), bf16)
 
@@ -340,6 +345,28 @@
         return 0
 
     lax.fori_loop(0, FACES, own1, 0)
+
+    column = column_of((COLS, C))
+    border = (column == 0) | (column == COLS - 1)
+
+    def inside(f, _):
+        for i in range(1, ROWS - 1):
+            h = silu(acc[f, i * COLS : (i + 1) * COLS])
+            hp[f, (i + 1) * COLS : (i + 2) * COLS] = jnp.where(border, 0.0, h).astype(bf16)
+        return 0
+
+    lax.fori_loop(0, FACES, inside, 0)
+
+    def own2(f, _):
+        z = from_west(conv_own(hp, tap2, f, 0)) + conv_own(hp, tap2, f, 1) + from_east(conv_own(hp, tap2, f, 2))
+        acc2[f] = z + b2[...]
+        return 0
+
+    lax.fori_loop(0, FACES, own2, 0)
+    for k, j in ((0, 0), (1, COLS - 1)):
+        for f in range(FACES):
+            line = [(FIRST + i, acc[f, i * COLS + j : i * COLS + j + 1, :]) for i in range(1, ROWS - 1)]
+            own_line[k, f * STACK : (f + 1) * STACK] = spread(line, STACK)
 
     for copy in sent:
         copy.wait_recv()
@@ -425,8 +452,6 @@
     near = jnp.where(place == FIRST - 1, low, jnp.where(place == FIRST + ROWS, high, near))
     near = near.astype(bf16)
 
-    column = column_of((COLS, C))
-
     def with_sides(z, f, q):
         west = zcol[0, pl.ds(f * STACK + q, 1), :]
         east = zcol[1, pl.ds(f * STACK + q, 1), :]
@@ -437,33 +462,56 @@
         at = pl.ds(pl.multiple_of(f * COLS, COLS), COLS)
         rows2[0, f] = silu(with_sides(zrow[0, at], f, 1)).astype(bf16)
         rows2[1, f] = silu(with_sides(zrow[1, at], f, STACK - 2)).astype(bf16)
-        for i in range(ROWS):
-            z = acc[f, i * COLS : (i + 1) * COLS]
-            if i == 0:
-                z = z + zrow[2, at]
-            if i == ROWS - 1:
-                z = z + zrow[3, at]
-            h = silu(with_sides(z, f, FIRST + i)).astype(bf16)
-            hp[f, (i + 1) * COLS : (i + 2) * COLS] = h
-            if i == 0:
-                rows2[2, f] = h
-            if i == ROWS - 1:
-                rows2[3, f] = h
+        rows2[2, f] = silu(with_sides(acc[f, 0:COLS] + zrow[2, at], f, FIRST)).astype(bf16)
+        z = acc[f, PIX - COLS : PIX] + zrow[3, at]
+        rows2[3, f] = silu(with_sides(z, f, FIRST + ROWS - 1)).astype(bf16)
         return 0
 
     lax.fori_loop(0, FACES, activate, 0)
+    place = lax.rem(lax.broadcasted_iota(i32, (half, C), 0), STACK)
+    between = (place > FIRST) & (place < FIRST + ROWS - 1)
+    west, east = [
+        jnp.where(between, silu(own_line[k] + zcol[k]), 0.0).astype(bf16) for k in range(2)
+    ]
+    tops, ends = [], []
     for f in range(FACES):
         face = g * FACES + f
         n, s = jnp.where(first, ns[0, face], f), jnp.where(last, ns[1, face], f)
-        hp[f, 0:COLS] = rows2[jnp.where(first, 2 * code[0, face], 0), n]
-        hp[f, PIX + COLS : PIX + 2 * COLS] = rows2[jnp.where(last, 1 + 2 * code[1, face], 1), s]
-    for k in range(2):
-        zcol[k] = along_rows(*[tap2(near[half * k : half * k + half], a, 2 * k) for a in range(3)])
+        tops.append(rows2[jnp.where(first, 2 * code[0, face], 0), n])
+        ends.append(rows2[jnp.where(last, 1 + 2 * code[1, face], 1), s])
+    top, end = [[rows2[k, f] for f in range(FACES)] for k in (2, 3)]
+    stacks = (tops + top, top + end, end + ends)
+    lines = ([near[0:half], west], [west, east], [near[half : 2 * half], east])
+    z_rows, v = [[], [], [], []], []
+    for b in range(3):
+        y = [tap2(jnp.concatenate(stacks[a] + lines[b], axis=0), a, b) for a in range(3)]
+        z_rows[0].append(y[0][0:ROW] + y[1][0:ROW])
+        z_rows[1].append(y[0][ROW : 2 * ROW])
+        z_rows[2].append(y[2][0:ROW])
+        z_rows[3].append(y[1][ROW : 2 * ROW] + y[2][ROW : 2 * ROW])
+        v.append([[x[2 * ROW + k * half : 2 * ROW + (k + 1) * half] for x in y] for k in range(2)])
+    for k, z in enumerate(z_rows):
+        zrow[k] = from_west(z[0]) + z[1] + from_east(z[2])
+    z_line[0] = along_rows(*[v[0][0][a] + v[1][0][a] for a in range(3)])
+    z_line[1] = along_rows(*v[0][1])
+    z_line[2] = along_rows(*v[2][1])
+    z_line[3] = along_rows(*[v[2][0][a] + v[1][1][a] for a in range(3)])
+
+    few = lax.broadcasted_iota(i32, (8, C), 0)
 
     def finish(f, _):
-        z = from_west(conv_own(hp, tap2, f, 0)) + conv_own(hp, tap2, f, 1) + from_east(conv_own(hp, tap2, f, 2))
+        at = pl.ds(pl.multiple_of(f * COLS, COLS), COLS)
         for i in range(ROWS):
-            feature = with_sides(z[i * COLS : (i + 1) * COLS], f, FIRST + i) + b2[...]
+            z = acc2[f, i * COLS : (i + 1) * COLS]
+            for k, row in enumerate((0, 1, ROWS - 2, ROWS - 1)):
+                if i == row:
+                    z = z + zrow[k, at]
+            line = [
+                jnp.broadcast_to(z_line[k, pl.ds(f * STACK + FIRST + i, 1), :], (8, C)) for k in range(4)
+            ]
+            west = jnp.where(few == 0, line[0], jnp.where(few == 1, line[1], 0.0))
+            east = jnp.where(few == 6, line[2], jnp.where(few == 7, line[3], 0.0))
+            feature = jnp.concatenate([z[0:8] + west, z[8 : COLS - 8], z[COLS - 8 :] + east], axis=0)
             p = pf[f, i * COLS : (i + 1) * COLS, 0:C]
             denoised = skip_gain * p + output_gain * feature
             out[f, i] = (p + step_ratio * (p - denoised)).astype(bf16)
@@ -489,6 +537,9 @@
         + [
             pltpu.VMEM((FACES, PIX, WIDE), f32),
             pltpu.VMEM((FACES, PIX, C), f32),
+            pltpu.VMEM((FACES, PIX, C), f32),
+            pltpu.VMEM((2, FACES * STACK, C), f32),
+            pltpu.VMEM((4, FACES * STACK, C), f32),
             pltpu.VMEM((FACES, PIX + 2 * COLS, WIDE), bf16),
             pltpu.VMEM((FACES, PIX + 2 * COLS, C), bf16),
             pltpu.VMEM((FACES * COLS, WIDE), bf16),

time: 27.5 us -> 26.8 us (0.975)
  Pallas kernels: 26.6 us -> 25.9 us
    pallas_call x1, Pallas kernels: 26.6 us -> 25.9 us  [on_device(): pl.pallas_call(functools.partial(kernel, groups, tiles), out_shape=jax.Sh...]
where the time goes in v4:
time: 26.8 us; the launch traced here: 26.6 us
  Pallas kernels  25.9 us (97%)
  local copies, waits for them, and re-layouts  0.75 us (3%)
    pallas_call x1, Pallas kernels, on_device(): pl.pallas_call(functools.partial(kernel, groups, tiles), out_shape=jax.Sh...  25.9 us
    unnamed x1, local copies, waits for them, and re-layouts  0.75 us

profile of v4, /device:TPU:1, one launch (start us, length us, event | category | flops | bytes accessed | tf_op | source)
XLA Modules:
  0.0 26.6 jit_solution(10292350424380530344)
XLA Ops:
  0.0 25.9 %shard_map.100 = bf16[3,8,32,192]{3,2,1,0:T(8,128)(2,1)S(1)} custom-call(bf16[3,8,32,192]{3,2,1,0:T(8,128)(2,1)} %sample_hbm.1, bf16[3,8,32,192]{3,2,1,0:T(8,128)(2,1)} %noise_hbm.1, bf16[3,1,4,192]{3,2,1,0:T(4,128)(2,1)} %coarse_hbm.1, s32[2,12]{1,0:T(2,128)} %bitcast.8, s32[2,12]{1,0:T(2,128)} %bitcast.9, s32[4,12]{1,0:T(4,128)} %bitcast.7, ...), custom_call_target="tpu_custom_call" | custom-call | tf_op jit(solution)/shard_map/pallas_call | solution.py:529
  25.9 0.7 %copy.12 = bf16[3,8,32,192]{3,2,1,0:T(8,128)(2,1)} copy(bf16[3,8,32,192]{3,2,1,0:T(8,128)(2,1)S(1)} %shard_map.100) | data formatting | bytes 589824

commit v5 on v4

--- a/solution.py
+++ b/solution.py
@@ -27,8 +27,10 @@
 SIDES = 2 * FACES
 WIDE = 256
 
-BLOCKS = 12
-OUTER, INNER, OVER, UNDER, EMPTY = 1, 4, 7, 9, 11
+BLOCKS = 6
+FACE, OVER, UNDER = 1, 4, 5
+LINE = 384
+CORNER = 4 * FACES
 STACK = 16
 FIRST = 4
 
@@ -68,6 +70,20 @@
     for at, row in rows:
         out = jnp.where(place == at, jnp.broadcast_to(row, (count, width)), out)
     return out
+
+
+def pack(outer, inner):
+    rest = outer[:, 128:WIDE] + pltpu.roll(inner[:, 128:WIDE], 64, 1)
+    return jnp.concatenate([outer[:, 0:128], rest, inner[:, 0:128]], axis=1).astype(bf16)
+
+
+def unpack_outer(y):
+    lane = lax.broadcasted_iota(i32, y.shape, 1)
+    return jnp.where(lane < LINE // 2, y, 0.0)
+
+
+def unpack_inner(y):
+    return unpack_outer(jnp.concatenate([y[:, 128:], pltpu.roll(y[:, 0:128], 64, 1)], axis=1))
 
 
 def kernel(
@@ -123,6 +139,14 @@
     C = acc.shape[2]
     lines = groups * BLOCKS * 16
 
+    barrier = pltpu.get_barrier_semaphore()
+    for d in (2, 1, 3, 0):
+        for k, there in enumerate((t, above, below)):
+            if d or k:
+                pl.semaphore_signal(
+                    barrier, inc=1, device_id=(lax.rem(g + d, groups), there), device_id_type=MESH
+                )
+
     loads = [
         pltpu.make_async_copy(src, dst, load_sem.at[i])
         for i, (src, dst) in enumerate(
@@ -143,14 +167,6 @@
     for copy in loads[:6]:
         copy.start()
 
-    barrier = pltpu.get_barrier_semaphore()
-    for d in (2, 1, 3, 0):
-        for k, there in enumerate((t, above, below)):
-            if d or k:
-                pl.semaphore_signal(
-                    barrier, inc=1, device_id=(lax.rem(g + d, groups), there), device_id_type=MESH
-                )
-
     for f in range(FACES):
         zero_row = jnp.zeros((COLS, WIDE), bf16)
         xp[f, 0:COLS] = zero_row
@@ -159,8 +175,6 @@
         pf[f, :, 128:WIDE] = jnp.zeros((PIX, WIDE - 128), f32)
         hp[f, 0 : 2 * COLS] = jnp.zeros((2 * COLS, C), bf16)
         hp[f, PIX : PIX + 2 * COLS] = jnp.zeros((2 * COLS, C), bf16)
-    for d in range(groups):
-        cols[d, EMPTY] = jnp.zeros((16, WIDE), bf16)
 
     for copy in loads[:3]:
         copy.wait()
@@ -172,31 +186,31 @@
         for r in range(2):
             rows1[2, f, r] = xp[f, (1 + r) * COLS : (2 + r) * COLS]
             rows1[3, f, r] = xp[f, PIX - COLS + r * COLS : PIX + r * COLS]
-    raw, tops, ends = [], [], []
+    raw, tops, ends = [([], []) for _ in range(3)]
+    blank = jnp.zeros((COARSE, WIDE - C), f32)
     for f in range(FACES):
         c = coarse[f, 0].astype(f32)
-        c = jnp.concatenate([jnp.zeros((COARSE, WIDE - C), f32), c], axis=1)
+        line = jnp.concatenate([c, blank], axis=1)
+        c = jnp.concatenate([blank, c], axis=1)
         each = [c[j : j + 1] for j in range(COARSE)]
-        raw += [(4 * f + j, each[j]) for j in range(COARSE)]
-        edges = [(24 + 2 * f, each[0]), (25 + 2 * f, each[COARSE - 1])]
         wide = jnp.concatenate([jnp.broadcast_to(e, (UP, WIDE)) for e in each], axis=0).astype(bf16)
         up[f * COLS : (f + 1) * COLS] = wide
         rows1[2, f, 2] = wide
         rows1[3, f, 2] = wide
-        tops += edges
-        ends += edges
-        for k, block, j in ((0, OUTER, 0), (3, OUTER, COLS - 1), (1, INNER, 1), (2, INNER, COLS - 2)):
-            line = [pf[f, i * COLS + j : i * COLS + j + 1, :] * input_gain for i in range(ROWS)]
-            half = spread(list(enumerate(line)), ROWS)
-            if k in (0, 1):
-                lower = half
-            else:
-                cols[g, block + f] = jnp.concatenate([lower, half], axis=0).astype(bf16)
-            tops += [(8 * f + 2 * k + r, line[r]) for r in range(2)]
-            ends += [(8 * f + 2 * k + r, line[ROWS - 2 + r]) for r in range(2)]
-    cols[g, 0] = spread(raw, 16).astype(bf16)
-    corner[0] = spread(tops, 32).astype(bf16).reshape(2, 16, WIDE)
-    corner[1] = spread(ends, 32).astype(bf16).reshape(2, 16, WIDE)
+        for inner, j in ((0, 0), (1, COARSE - 1)):
+            raw[inner].append((f, line[j : j + 1]))
+            tops[inner].append((CORNER + f, line[j : j + 1]))
+            ends[inner].append((CORNER + f, line[j : j + 1]))
+        halves = ([], [])
+        for inner, high, j in ((0, 0, 0), (0, 1, COLS - 1), (1, 0, 1), (1, 1, COLS - 2)):
+            line_j = [pf[f, i * COLS + j : i * COLS + j + 1, :] * input_gain for i in range(ROWS)]
+            halves[inner].append(spread(list(enumerate(line_j)), ROWS))
+            tops[inner].extend((4 * f + 2 * high + r, line_j[r]) for r in range(2))
+            ends[inner].extend((4 * f + 2 * high + r, line_j[ROWS - 2 + r]) for r in range(2))
+        cols[g, FACE + f] = pack(*[jnp.concatenate(h, axis=0) for h in halves])
+    cols[g, 0] = pack(*[spread(x, 16) for x in raw])
+    corner[0] = pack(*[spread(x, 16) for x in tops])
+    corner[1] = pack(*[spread(x, 16) for x in ends])
 
     sent = []
 
@@ -214,8 +228,8 @@
         )
 
     table = cols.at[g, pl.ds(0, OVER)]
-    over = cols.at[g, pl.ds(OVER, 2)]
-    under = cols.at[g, pl.ds(UNDER, 2)]
+    over = cols.at[g, OVER]
+    under = cols.at[g, UNDER]
     for d in (2, 1, 3):
         far = lax.rem(g + d, groups)
         add(corner.at[0], under, (far, above))
@@ -248,22 +262,22 @@
     def write_pick(at, face, column, beyond):
         group, f = split(face)
         base = group * (BLOCKS * 16)
-        inner = ((column == 1) | (column == 2)).astype(i32)
+        inner = (column == 1) | (column == 2)
         high = (column >= 2).astype(i32)
 
         def line(ff, row):
             if row < 0:
-                return base + OVER * 16 + ff * 8 + column * 2 + 2 + row
+                return base + OVER * 16 + ff * 4 + high * 2 + 2 + row
             if row >= ROWS:
-                return base + UNDER * 16 + ff * 8 + column * 2 + row - ROWS
-            return base + (OUTER + inner * (INNER - OUTER) + ff) * 16 + high * 8 + row
+                return base + UNDER * 16 + ff * 4 + high * 2 + row - ROWS
+            return base + (FACE + ff) * 16 + high * 8 + row
 
         def condition(ff, row):
             if row < 0:
-                return base + OVER * 16 + 24 + ff * 2 + high
+                return base + OVER * 16 + CORNER + ff
             if row >= ROWS:
-                return base + UNDER * 16 + 24 + ff * 2 + high
-            return base + ff * COARSE + high * (COARSE - 1)
+                return base + UNDER * 16 + CORNER + ff
+            return base + ff
 
         n, s = ns[0, face], ns[1, face]
         flip_n, flip_s = code[0, face] == 1, code[1, face] == 1
@@ -285,7 +299,9 @@
             ):
                 target = jnp.where(place == q, value, target)
             at = pl.multiple_of(at, STACK)
-            pick[part, pl.ds(at, STACK), :] = jnp.where(lane == target, 1.0, 0.0).astype(bf16)
+            second = high == 1 if part else inner
+            for k, chosen in ((0, jnp.where(second, -1, target)), (1, jnp.where(second, target, -1))):
+                pick[part, k, pl.ds(at, STACK), :] = jnp.where(lane == chosen, 1.0, 0.0).astype(bf16)
 
     def pick_side(n, _):
         side = (n >= FACES).astype(i32)
@@ -297,12 +313,12 @@
         at_east = column == 3
         write_pick(n * STACK, near, column, True)
         write_pick(
-            (SIDES + n) * STACK,
+            (2 * SIDES + n) * STACK,
             jnp.where(at_west, west_face, near),
             jnp.where(at_west, west_column, 2),
             at_west,
         )
-        write_pick((2 * SIDES + n) * STACK, near, column, False)
+        write_pick((SIDES + n) * STACK, near, column, False)
         write_pick(
             (3 * SIDES + n) * STACK,
             jnp.where(at_east, east_face, near),
@@ -368,10 +384,8 @@
             line = [(FIRST + i, acc[f, i * COLS + j : i * COLS + j + 1, :]) for i in range(1, ROWS - 1)]
             own_line[k, f * STACK : (f + 1) * STACK] = spread(line, STACK)
 
-    for copy in sent:
+    for copy in sent[-2:]:
         copy.wait_recv()
-    table = cols[...].reshape(lines, WIDE)
-    picked = [dot(pick[part], table).astype(bf16) for part in range(2)]
 
     tops, ends, after, before = [], [], [], []
     for f in range(FACES):
@@ -402,46 +416,49 @@
         landed(0, 1) + landed(1, 0),
         after + landed(1, 1) + ends,
     )
+    taps = (tap1, tap1_coarse)
+    z_rows = [[], [], [], []]
+    for b in range(3):
+        y = [
+            sum(tap(jnp.concatenate([r[k] for r in stacks[a]], axis=0), a, b) for k, tap in enumerate(taps))
+            for a in range(3)
+        ]
+        z_rows[0].append(y[0][0:ROW] + y[1][0:ROW] + y[2][0:ROW])
+        z_rows[1].append(y[0][2 * ROW :] + y[1][ROW:] + y[2][ROW : 2 * ROW])
+        z_rows[2].append(y[0][ROW : 2 * ROW])
+        z_rows[3].append(y[2][2 * ROW :])
+    for k, z in enumerate(z_rows):
+        z = from_west(z[0]) + z[1] + from_east(z[2])
+        zrow[k] = z if k >= 2 else z + b1[...]
+
+    for copy in sent[:-2]:
+        copy.wait_recv()
+    table = cols[...].reshape(lines, LINE)
     half = FACES * STACK
     sides = SIDES * STACK
-    z_over, z_under, z_top, z_end = [], [], [], []
-    v_side, v_near = [[], []], []
+    y = unpack_outer(dot(pick[0, 0], table[:, 0:WIDE]))
+    z = unpack_inner(dot(pick[0, 1, 2 * sides :], table[:, LINE - WIDE :]))
+    picked = [jnp.concatenate([y[0 : 2 * sides], y[2 * sides :] + z], axis=0).astype(bf16)]
+    y = unpack_outer(dot(pick[1, 0], table[:, 0:WIDE]))
+    z = unpack_inner(dot(pick[1, 1], table[:, LINE - WIDE :]))
+    picked.append(pltpu.roll(y + z, 64, 1).astype(bf16))
+
+    v_side, v_near = [], []
     for b in range(3):
-        over, under, near = 0.0, 0.0, []
-        for a in range(3):
-            y = 0.0
-            for part, tap in enumerate((tap1, tap1_coarse)):
-                chosen = picked[part]
-                if b == 0:
-                    extra = [chosen[0:half], chosen[sides : 2 * sides]]
-                elif b == 1:
-                    extra = [chosen[2 * sides : 3 * sides]]
-                else:
-                    extra = [chosen[half : 2 * half], chosen[3 * sides : 4 * sides]]
-                y = y + tap(jnp.concatenate([r[part] for r in stacks[a]] + extra, axis=0), a, b)
-            if a == 0:
-                over = over + y[0:ROW]
-                z_top.append(y[ROW : 2 * ROW])
-                under = under + y[2 * ROW : 3 * ROW]
-            elif a == 1:
-                over = over + y[0:ROW]
-                under = under + y[ROW : 2 * ROW]
+        lines_b = []
+        for chosen in picked:
+            if b == 0:
+                beside = [chosen[0:half], chosen[2 * sides : 3 * sides]]
+            elif b == 1:
+                beside = [chosen[sides : 2 * sides]]
             else:
-                over = over + y[0:ROW]
-                under = under + y[ROW : 2 * ROW]
-                z_end.append(y[2 * ROW : 3 * ROW])
-            rest = y[len(stacks[a]) * COLS :]
-            if b != 1:
-                v_side[b // 2].append(rest[0:half])
-                rest = rest[half:]
-            near.append(rest)
-        z_over.append(over)
-        z_under.append(under)
-        v_near.append(near)
-
-    for k, z in enumerate((z_over, z_under, z_top, z_end)):
-        z = from_west(z[0]) + z[1] + from_east(z[2])
-        zrow[k] = z if k >= 2 else z + b1[...]
+                beside = [chosen[half : 2 * half], chosen[3 * sides :]]
+            lines_b.append(jnp.concatenate(beside, axis=0))
+        y = [sum(tap(x, a, b) for tap, x in zip(taps, lines_b)) for a in range(3)]
+        if b != 1:
+            v_side.append([x[0:half] for x in y])
+            y = [x[half:] for x in y]
+        v_near.append(y)
     for k in range(2):
         zcol[k] = along_rows(*v_side[k])
     near = along_rows(*[v_near[0][a] + v_near[1][a] + v_near[2][a] for a in range(3)]) + b1[...]
@@ -544,11 +561,11 @@
             pltpu.VMEM((FACES, PIX + 2 * COLS, C), bf16),
             pltpu.VMEM((FACES * COLS, WIDE), bf16),
             pltpu.VMEM((3, FACES * COLS, C), f32),
-            pltpu.VMEM((groups, BLOCKS, 16, WIDE), bf16),
-            pltpu.VMEM((2, 2, 16, WIDE), bf16),
+            pltpu.VMEM((groups, BLOCKS, 16, LINE), bf16),
+            pltpu.VMEM((2, 16, LINE), bf16),
             pltpu.VMEM((4, FACES, 3, COLS, WIDE), bf16),
             pltpu.VMEM((4, FACES, COLS, C), bf16),
-            pltpu.VMEM((2, 4 * SIDES * STACK, groups * BLOCKS * 16), bf16),
+            pltpu.VMEM((2, 2, 4 * SIDES * STACK, groups * BLOCKS * 16), bf16),
             pltpu.VMEM((2, FACES * STACK, C), f32),
             pltpu.VMEM((4, FACES * COLS, C), f32),
             pltpu.SemaphoreType.DMA((len(operands),)),

time: 26.8 us -> 25.9 us (0.966)
  Pallas kernels: 25.9 us -> 25 us
    pallas_call x1, Pallas kernels: 25.9 us -> 25 us  [on_device(): pl.pallas_call(functools.partial(kernel, groups, tiles), out_shape=jax.Sh...]
where the time goes in v5:
time: 25.9 us; the launch traced here: 25.8 us
  Pallas kernels  25 us (97%)
  local copies, waits for them, and re-layouts  0.75 us (3%)
    pallas_call x1, Pallas kernels, on_device(): pl.pallas_call(functools.partial(kernel, groups, tiles), out_shape=jax.Sh...  25 us
    unnamed x1, local copies, waits for them, and re-layouts  0.75 us

profile of v5, /device:TPU:1, one launch (start us, length us, event | category | flops | bytes accessed | tf_op | source)
XLA Modules:
  0.0 25.8 jit_solution(12926616000263965934)
XLA Ops:
  0.0 25.0 %shard_map.100 = bf16[3,8,32,192]{3,2,1,0:T(8,128)(2,1)S(1)} custom-call(bf16[3,8,32,192]{3,2,1,0:T(8,128)(2,1)} %sample_hbm.1, bf16[3,8,32,192]{3,2,1,0:T(8,128)(2,1)} %noise_hbm.1, bf16[3,1,4,192]{3,2,1,0:T(4,128)(2,1)} %coarse_hbm.1, s32[2,12]{1,0:T(2,128)} %bitcast.8, s32[2,12]{1,0:T(2,128)} %bitcast.9, s32[4,12]{1,0:T(4,128)} %bitcast.7, ...), custom_call_target="tpu_custom_call" | custom-call | tf_op jit(solution)/shard_map/pallas_call | solution.py:546
  25.0 0.7 %copy.12 = bf16[3,8,32,192]{3,2,1,0:T(8,128)(2,1)} copy(bf16[3,8,32,192]{3,2,1,0:T(8,128)(2,1)S(1)} %shard_map.100) | data formatting | bytes 589824

commit v6 on v5

--- a/solution.py
+++ b/solution.py
@@ -17,6 +17,7 @@
 skip_gain = 0.5
 output_gain = 0.7071067811865476
 step_ratio = -0.4
+feature_gain = -step_ratio * output_gain
 
 UP = 8
 FACES = 3
@@ -375,7 +376,12 @@
 
     def own2(f, _):
         z = from_west(conv_own(hp, tap2, f, 0)) + conv_own(hp, tap2, f, 1) + from_east(conv_own(hp, tap2, f, 2))
-        acc2[f] = z + b2[...]
+        p = pf[f, :, 0:C]
+        denoised = skip_gain * p + output_gain * (z + b2[...])
+        z = p + step_ratio * (p - denoised)
+        acc2[f] = z
+        for i in range(2, ROWS - 2):
+            out[f, i] = z[i * COLS : (i + 1) * COLS].astype(bf16)
         return 0
 
     lax.fori_loop(0, FACES, own2, 0)
@@ -519,19 +525,19 @@
     def finish(f, _):
         at = pl.ds(pl.multiple_of(f * COLS, COLS), COLS)
         for i in range(ROWS):
-            z = acc2[f, i * COLS : (i + 1) * COLS]
-            for k, row in enumerate((0, 1, ROWS - 2, ROWS - 1)):
-                if i == row:
-                    z = z + zrow[k, at]
             line = [
                 jnp.broadcast_to(z_line[k, pl.ds(f * STACK + FIRST + i, 1), :], (8, C)) for k in range(4)
             ]
             west = jnp.where(few == 0, line[0], jnp.where(few == 1, line[1], 0.0))
             east = jnp.where(few == 6, line[2], jnp.where(few == 7, line[3], 0.0))
-            feature = jnp.concatenate([z[0:8] + west, z[8 : COLS - 8], z[COLS - 8 :] + east], axis=0)
-            p = pf[f, i * COLS : (i + 1) * COLS, 0:C]
-            denoised = skip_gain * p + output_gain * feature
-            out[f, i] = (p + step_ratio * (p - denoised)).astype(bf16)
+            r = i * COLS
+            if 2 <= i < ROWS - 2:
+                out[f, i, 0:8] = (acc2[f, r : r + 8] + feature_gain * west).astype(bf16)
+                out[f, i, COLS - 8 :] = (acc2[f, r + COLS - 8 : r + COLS] + feature_gain * east).astype(bf16)
+                continue
+            z = zrow[i if i < 2 else i - ROWS + 4, at]
+            z = jnp.concatenate([z[0:8] + west, z[8 : COLS - 8], z[COLS - 8 :] + east], axis=0)
+            out[f, i] = (acc2[f, r : r + COLS] + feature_gain * z).astype(bf16)
         return 0
 
     lax.fori_loop(0, FACES, finish, 0)

time: 25.9 us -> 25.8 us (level)
  no operation moved by 1% of the time
where the time goes in v6:
time: 25.8 us; the launch traced here: 25.6 us
  Pallas kernels  24.9 us (97%)
  local copies, waits for them, and re-layouts  0.75 us (3%)
    pallas_call x1, Pallas kernels, on_device(): pl.pallas_call(functools.partial(kernel, groups, tiles), out_shape=jax.Sh...  24.9 us
    unnamed x1, local copies, waits for them, and re-layouts  0.75 us

profile of v6, /device:TPU:1, one launch (start us, length us, event | category | flops | bytes accessed | tf_op | source)
XLA Modules:
  0.0 25.6 jit_solution(18238676959737374283)
XLA Ops:
  0.0 24.9 %shard_map.100 = bf16[3,8,32,192]{3,2,1,0:T(8,128)(2,1)S(1)} custom-call(bf16[3,8,32,192]{3,2,1,0:T(8,128)(2,1)} %sample_hbm.1, bf16[3,8,32,192]{3,2,1,0:T(8,128)(2,1)} %noise_hbm.1, bf16[3,1,4,192]{3,2,1,0:T(4,128)(2,1)} %coarse_hbm.1, s32[2,12]{1,0:T(2,128)} %bitcast.8, s32[2,12]{1,0:T(2,128)} %bitcast.9, s32[4,12]{1,0:T(4,128)} %bitcast.7, ...), custom_call_target="tpu_custom_call" | custom-call | tf_op jit(solution)/shard_map/pallas_call | solution.py:552
  24.9 0.7 %copy.12 = bf16[3,8,32,192]{3,2,1,0:T(8,128)(2,1)} copy(bf16[3,8,32,192]{3,2,1,0:T(8,128)(2,1)S(1)} %shard_map.100) | data formatting | bytes 589824

commit v7 on v6

--- a/solution.py
+++ b/solution.py
@@ -302,7 +302,7 @@
             at = pl.multiple_of(at, STACK)
             second = high == 1 if part else inner
             for k, chosen in ((0, jnp.where(second, -1, target)), (1, jnp.where(second, target, -1))):
-                pick[part, k, pl.ds(at, STACK), :] = jnp.where(lane == chosen, 1.0, 0.0).astype(bf16)
+                pick[k, part, pl.ds(at, STACK), :] = jnp.where(lane == chosen, 1.0, 0.0).astype(bf16)
 
     def pick_side(n, _):
         side = (n >= FACES).astype(i32)
@@ -442,12 +442,11 @@
     table = cols[...].reshape(lines, LINE)
     half = FACES * STACK
     sides = SIDES * STACK
-    y = unpack_outer(dot(pick[0, 0], table[:, 0:WIDE]))
-    z = unpack_inner(dot(pick[0, 1, 2 * sides :], table[:, LINE - WIDE :]))
-    picked = [jnp.concatenate([y[0 : 2 * sides], y[2 * sides :] + z], axis=0).astype(bf16)]
-    y = unpack_outer(dot(pick[1, 0], table[:, 0:WIDE]))
-    z = unpack_inner(dot(pick[1, 1], table[:, LINE - WIDE :]))
-    picked.append(pltpu.roll(y + z, 64, 1).astype(bf16))
+    y = unpack_outer(dot(pick[0].reshape(8 * sides, lines), table[:, 0:WIDE]))
+    z = unpack_inner(dot(pick[1].reshape(8 * sides, lines)[2 * sides :], table[:, LINE - WIDE :]))
+    picked = [jnp.concatenate([y[0 : 2 * sides], y[2 * sides : 4 * sides] + z[0 : 2 * sides]], axis=0)]
+    picked.append(pltpu.roll(y[4 * sides :] + z[2 * sides :], 64, 1))
+    picked = [x.astype(bf16) for x in picked]
 
     v_side, v_near = [], []
     for b in range(3):
@@ -481,16 +480,16 @@
         z = z + jnp.where(column == 0, jnp.broadcast_to(west, z.shape), 0.0)
         return z + jnp.where(column == COLS - 1, jnp.broadcast_to(east, z.shape), 0.0)
 
-    def activate(f, _):
-        at = pl.ds(pl.multiple_of(f * COLS, COLS), COLS)
+    def activate(f):
+        at = pl.ds(f * COLS, COLS)
         rows2[0, f] = silu(with_sides(zrow[0, at], f, 1)).astype(bf16)
         rows2[1, f] = silu(with_sides(zrow[1, at], f, STACK - 2)).astype(bf16)
         rows2[2, f] = silu(with_sides(acc[f, 0:COLS] + zrow[2, at], f, FIRST)).astype(bf16)
         z = acc[f, PIX - COLS : PIX] + zrow[3, at]
         rows2[3, f] = silu(with_sides(z, f, FIRST + ROWS - 1)).astype(bf16)
-        return 0
-
-    lax.fori_loop(0, FACES, activate, 0)
+
+    for f in range(FACES):
+        activate(f)
     place = lax.rem(lax.broadcasted_iota(i32, (half, C), 0), STACK)
     between = (place > FIRST) & (place < FIRST + ROWS - 1)
     west, east = [
@@ -522,8 +521,8 @@
 
     few = lax.broadcasted_iota(i32, (8, C), 0)
 
-    def finish(f, _):
-        at = pl.ds(pl.multiple_of(f * COLS, COLS), COLS)
+    def finish(f):
+        at = pl.ds(f * COLS, COLS)
         for i in range(ROWS):
             line = [
                 jnp.broadcast_to(z_line[k, pl.ds(f * STACK + FIRST + i, 1), :], (8, C)) for k in range(4)
@@ -538,9 +537,9 @@
             z = zrow[i if i < 2 else i - ROWS + 4, at]
             z = jnp.concatenate([z[0:8] + west, z[8 : COLS - 8], z[COLS - 8 :] + east], axis=0)
             out[f, i] = (acc2[f, r : r + COLS] + feature_gain * z).astype(bf16)
-        return 0
-
-    lax.fori_loop(0, FACES, finish, 0)
+
+    for f in range(FACES):
+        finish(f)
     for copy in sent:
         copy.wait_send()
 

time: 25.8 us -> 25.5 us (0.988)
  Pallas kernels: 24.9 us -> 24.6 us
    pallas_call x1, Pallas kernels: 24.9 us -> 24.6 us  [on_device(): pl.pallas_call(functools.partial(kernel, groups, tiles), out_shape=jax.Sh...]
where the time goes in v7:
time: 25.5 us; the launch traced here: 25.4 us
  Pallas kernels  24.6 us (96%)
  local copies, waits for them, and re-layouts  0.75 us (3%)
    pallas_call x1, Pallas kernels, on_device(): pl.pallas_call(functools.partial(kernel, groups, tiles), out_shape=jax.Sh...  24.6 us
    unnamed x1, local copies, waits for them, and re-layouts  0.75 us

profile of v7, /device:TPU:1, one launch (start us, length us, event | category | flops | bytes accessed | tf_op | source)
XLA Modules:
  0.0 25.4 jit_solution(2536932685937855938)
XLA Ops:
  0.0 24.6 %shard_map.100 = bf16[3,8,32,192]{3,2,1,0:T(8,128)(2,1)S(1)} custom-call(bf16[3,8,32,192]{3,2,1,0:T(8,128)(2,1)} %sample_hbm.1, bf16[3,8,32,192]{3,2,1,0:T(8,128)(2,1)} %noise_hbm.1, bf16[3,1,4,192]{3,2,1,0:T(4,128)(2,1)} %coarse_hbm.1, s32[2,12]{1,0:T(2,128)} %bitcast.8, s32[2,12]{1,0:T(2,128)} %bitcast.9, s32[4,12]{1,0:T(4,128)} %bitcast.7, ...), custom_call_target="tpu_custom_call" | custom-call | tf_op jit(solution)/shard_map/pallas_call | solution.py:551
  24.6 0.7 %copy.12 = bf16[3,8,32,192]{3,2,1,0:T(8,128)(2,1)} copy(bf16[3,8,32,192]{3,2,1,0:T(8,128)(2,1)S(1)} %shard_map.100) | data formatting | bytes 589824

commit v8 on v7

--- a/solution.py
+++ b/solution.py
@@ -85,6 +85,10 @@
 
 def unpack_inner(y):
     return unpack_outer(jnp.concatenate([y[:, 128:], pltpu.roll(y[:, 0:128], 64, 1)], axis=1))
+
+
+def widened(each):
+    return jnp.concatenate([jnp.broadcast_to(e, (UP, WIDE)) for e in each], axis=0).astype(bf16)
 
 
 def kernel(
@@ -122,6 +126,7 @@
     cclass,
     cols,
     corner,
+    craw,
     rows1,
     rows2,
     pick,
@@ -188,13 +193,15 @@
             rows1[2, f, r] = xp[f, (1 + r) * COLS : (2 + r) * COLS]
             rows1[3, f, r] = xp[f, PIX - COLS + r * COLS : PIX + r * COLS]
     raw, tops, ends = [([], []) for _ in range(3)]
+    all_raw = []
     blank = jnp.zeros((COARSE, WIDE - C), f32)
     for f in range(FACES):
         c = coarse[f, 0].astype(f32)
         line = jnp.concatenate([c, blank], axis=1)
         c = jnp.concatenate([blank, c], axis=1)
         each = [c[j : j + 1] for j in range(COARSE)]
-        wide = jnp.concatenate([jnp.broadcast_to(e, (UP, WIDE)) for e in each], axis=0).astype(bf16)
+        wide = widened(each)
+        all_raw += [(f * COARSE + j, each[j]) for j in range(COARSE)]
         up[f * COLS : (f + 1) * COLS] = wide
         rows1[2, f, 2] = wide
         rows1[3, f, 2] = wide
@@ -210,6 +217,7 @@
             ends[inner].extend((4 * f + 2 * high + r, line_j[ROWS - 2 + r]) for r in range(2))
         cols[g, FACE + f] = pack(*[jnp.concatenate(h, axis=0) for h in halves])
     cols[g, 0] = pack(*[spread(x, 16) for x in raw])
+    craw[2] = spread(all_raw, 16).astype(bf16)
     corner[0] = pack(*[spread(x, 16) for x in tops])
     corner[1] = pack(*[spread(x, 16) for x in ends])
 
@@ -238,8 +246,11 @@
         add(table, table, (far, t))
     add(corner.at[0], under, (g, above))
     add(corner.at[1], over, (g, below))
-    add(rows1.at[2], rows1.at[1], (g, above))
-    add(rows1.at[3], rows1.at[0], (g, below))
+    both = pl.ds(0, 2)
+    add(rows1.at[2, :, both], rows1.at[1, :, both], (g, above))
+    add(rows1.at[3, :, both], rows1.at[0, :, both], (g, below))
+    add(craw.at[2], craw.at[1], (g, above))
+    add(craw.at[2], craw.at[0], (g, below))
 
     pl.semaphore_wait(barrier, 3 * groups - 1)
     for copy in sent:
@@ -390,8 +401,12 @@
             line = [(FIRST + i, acc[f, i * COLS + j : i * COLS + j + 1, :]) for i in range(1, ROWS - 1)]
             own_line[k, f * STACK : (f + 1) * STACK] = spread(line, STACK)
 
-    for copy in sent[-2:]:
+    for copy in sent[-4:]:
         copy.wait_recv()
+    for k in range(2):
+        c = craw[k].astype(f32)
+        for f in range(FACES):
+            rows1[k, f, 2] = widened([c[n : n + 1] for n in range(f * COARSE, (f + 1) * COARSE)])
 
     tops, ends, after, before = [], [], [], []
     for f in range(FACES):
@@ -437,7 +452,7 @@
         z = from_west(z[0]) + z[1] + from_east(z[2])
         zrow[k] = z if k >= 2 else z + b1[...]
 
-    for copy in sent[:-2]:
+    for copy in sent[:-4]:
         copy.wait_recv()
     table = cols[...].reshape(lines, LINE)
     half = FACES * STACK
@@ -568,14 +583,15 @@
             pltpu.VMEM((3, FACES * COLS, C), f32),
             pltpu.VMEM((groups, BLOCKS, 16, LINE), bf16),
             pltpu.VMEM((2, 16, LINE), bf16),
+            pltpu.VMEM((3, 16, WIDE), bf16),
             pltpu.VMEM((4, FACES, 3, COLS, WIDE), bf16),
             pltpu.VMEM((4, FACES, COLS, C), bf16),
             pltpu.VMEM((2, 2, 4 * SIDES * STACK, groups * BLOCKS * 16), bf16),
             pltpu.VMEM((2, FACES * STACK, C), f32),
             pltpu.VMEM((4, FACES * COLS, C), f32),
             pltpu.SemaphoreType.DMA((len(operands),)),
-            pltpu.SemaphoreType.DMA((13,)),
-            pltpu.SemaphoreType.DMA((13,)),
+            pltpu.SemaphoreType.DMA((15,)),
+            pltpu.SemaphoreType.DMA((15,)),
         ],
         compiler_params=pltpu.CompilerParams(
             collective_id=0, has_side_effects=True, vmem_limit_bytes=32 * 2**20

time: 25.5 us -> 24.9 us (0.976)
  the two profiles are of different devices: /device:TPU:1 before, /device:TPU:4 now
where the time goes in v8:
time: 24.9 us; the launch traced here: 24.7 us
  Pallas kernels  23.9 us (96%)
  local copies, waits for them, and re-layouts  0.75 us (3%)
    pallas_call x1, Pallas kernels, on_device(): pl.pallas_call(functools.partial(kernel, groups, tiles), out_shape=jax.Sh...  23.9 us
    unnamed x1, local copies, waits for them, and re-layouts  0.75 us

profile of v8, /device:TPU:4, one launch (start us, length us, event | category | flops | bytes accessed | tf_op | source)
XLA Modules:
  0.0 24.7 jit_solution(12698651678690629567)
XLA Ops:
  0.0 23.9 %shard_map.100 = bf16[3,8,32,192]{3,2,1,0:T(8,128)(2,1)S(1)} custom-call(bf16[3,8,32,192]{3,2,1,0:T(8,128)(2,1)} %sample_hbm.1, bf16[3,8,32,192]{3,2,1,0:T(8,128)(2,1)} %noise_hbm.1, bf16[3,1,4,192]{3,2,1,0:T(4,128)(2,1)} %coarse_hbm.1, s32[2,12]{1,0:T(2,128)} %bitcast.8, s32[2,12]{1,0:T(2,128)} %bitcast.9, s32[4,12]{1,0:T(4,128)} %bitcast.7, ...), custom_call_target="tpu_custom_call" | custom-call | tf_op jit(solution)/shard_map/pallas_call | solution.py:566
  24.0 0.7 %copy.12 = bf16[3,8,32,192]{3,2,1,0:T(8,128)(2,1)} copy(bf16[3,8,32,192]{3,2,1,0:T(8,128)(2,1)S(1)} %shard_map.100) | data formatting | bytes 589824

commit v9 on v8

--- a/solution.py
+++ b/solution.py
@@ -61,7 +61,7 @@
 
 
 def silu(u):
-    return u / (1.0 + jnp.exp(-u))
+    return 0.5 * u * (1.0 + jnp.tanh(0.5 * u))
 
 
 def spread(rows, count):

time: 24.9 us -> 24.8 us (level)
  no operation moved by 1% of the time
where the time goes in v9:
time: 24.8 us; the launch traced here: 24.7 us
  Pallas kernels  23.9 us (96%)
  local copies, waits for them, and re-layouts  0.75 us (3%)
    pallas_call x1, Pallas kernels, on_device(): pl.pallas_call(functools.partial(kernel, groups, tiles), out_shape=jax.Sh...  23.9 us
    unnamed x1, local copies, waits for them, and re-layouts  0.75 us

profile of v9, /device:TPU:4, one launch (start us, length us, event | category | flops | bytes accessed | tf_op | source)
XLA Modules:
  0.0 24.7 jit_solution(11856072672026186708)
XLA Ops:
  0.0 23.9 %shard_map.100 = bf16[3,8,32,192]{3,2,1,0:T(8,128)(2,1)S(1)} custom-call(bf16[3,8,32,192]{3,2,1,0:T(8,128)(2,1)} %sample_hbm.1, bf16[3,8,32,192]{3,2,1,0:T(8,128)(2,1)} %noise_hbm.1, bf16[3,1,4,192]{3,2,1,0:T(4,128)(2,1)} %coarse_hbm.1, s32[2,12]{1,0:T(2,128)} %bitcast.8, s32[2,12]{1,0:T(2,128)} %bitcast.9, s32[4,12]{1,0:T(4,128)} %bitcast.7, ...), custom_call_target="tpu_custom_call" | custom-call | tf_op jit(solution)/shard_map/pallas_call | solution.py:566
  23.9 0.7 %copy.12 = bf16[3,8,32,192]{3,2,1,0:T(8,128)(2,1)} copy(bf16[3,8,32,192]{3,2,1,0:T(8,128)(2,1)S(1)} %shard_map.100) | data formatting | bytes 589824
